TPU v7x, 32 devices: a whole 2x2x4 slice. The times are simulated.
32 devices in a mesh: ctx: 8 (over z, y), ws: 4 (over x, core).
Axes of the slice: x: 2, y: 2, z: 4, core: 2. Of those that a mesh axis runs over, the one named last changes fastest.
Arguments:
- tokens: bfloat16 [4, 2048, 576], P('ws', 'ctx'), may hold values from -6 to 6
- attn_gain: bfloat16 [576], P('ws'), may hold values from 0.25 to 1.75
- query_weight: bfloat16 [576, 576], P('ws'), may hold values from -0.375 to 0.375
- key_weight: bfloat16 [576, 192], P('ws'), may hold values from -0.375 to 0.375
- value_weight: bfloat16 [576, 192], P('ws'), may hold values from -0.25 to 0.25
- output_weight: bfloat16 [576, 576], P('ws'), may hold values from -1 to 1
- ffn_gain: bfloat16 [576], P('ws'), may hold values from 0.25 to 1.75
- gate_weight: bfloat16 [576, 1536], P('ws'), may hold values from -0.25 to 0.25
- up_weight: bfloat16 [576, 1536], P('ws'), may hold values from -0.25 to 0.25
- down_weight: bfloat16 [1536, 576], P('ws'), may hold values from -0.21875 to 0.21875
- out_grad: bfloat16 [4, 2048, 576], P('ws', 'ctx'), may hold values from -6 to 6
Outputs:
- layer_out: bfloat16 [4, 2048, 576], P('ws', 'ctx')
- tokens_grad: bfloat16 [4, 2048, 576], P('ws', 'ctx')
- attn_gain_grad: float32 [576], P('ws')
- query_weight_grad: float32 [576, 576], P('ws')
- key_weight_grad: float32 [576, 192], P('ws')
- value_weight_grad: float32 [576, 192], P('ws')
- output_weight_grad: float32 [576, 576], P('ws')
- ffn_gain_grad: float32 [576], P('ws')
- gate_weight_grad: float32 [576, 1536], P('ws')
- up_weight_grad: float32 [576, 1536], P('ws')
- down_weight_grad: float32 [1536, 576], P('ws')
All inputs are finite; a program needn't handle non-finite values.
Results may differ from a plain program's by a relative error of at most 0.022.
Values may be sent and summed in bfloat16 or wider, within the bound.
No kernel may reach another device: no remote copies, remote signals or barrier semaphores. Data moves between devices by JAX's collectives and lax.ppermute only.
A program may use at most 128 MiB of HBM per device.

v0:
```python
import math

import jax
import jax.numpy as jnp
from jax import lax
from jax.sharding import PartitionSpec as P

H = 9
KV = 3
HD = 64


EPS = 1e-05
THETA = 100000.0
NEGATIVE = -1e30


def from_behind(array, axis, by):
    peers = lax.axis_size(axis)
    pairs = [(i, i + by) for i in range(peers) if 0 <= i + by < peers]
    return lax.ppermute(array, axis, pairs)


def passed_along(value, axis, steps):
    count = lax.axis_size(axis)
    pairs = [(source, (source + steps) % count) for source in range(count)]
    return lax.ppermute(value, axis, pairs)


def rms_scale(values, gain_vec):
    return values * lax.rsqrt(jnp.mean(values * values, -1, keepdims=True) + EPS) * gain_vec


def rope_tables(positions, head_width):
    half_width = head_width // 2
    frequency = jnp.exp(
        jnp.arange(half_width).astype(jnp.float32) * (-2.0 * math.log(THETA) / head_width)
    )
    angles = positions[:, None] * frequency[None, :]
    angles = jnp.concatenate([angles, angles], -1)
    return (jnp.cos(angles)[:, None, :], jnp.sin(angles)[:, None, :])


def rotate_pairs(values, cosine_table, sine_table):
    half_width = values.shape[-1] // 2
    turned = jnp.concatenate([-values[..., half_width:], values[..., :half_width]], -1)
    return values * cosine_table + turned * sine_table


def body(
    tokens,
    attn_gain,
    query_weight,
    key_weight,
    value_weight,
    output_weight,
    ffn_gain,
    gate_weight,
    up_weight,
    down_weight,
    out_grad,
):
    seq_count, block_rows, width = tokens.shape
    ctx_count = lax.axis_size("ctx")
    ctx_index = lax.axis_index("ctx")
    groups = H // KV
    kv_width = KV * HD
    group_rows = groups * block_rows
    (
        full_query,
        full_key,
        full_value,
        full_output,
        full_gate,
        full_up,
        full_down,
        gain_first,
        gain_second,
    ) = (
        lax.all_gather(query_weight, "ws", axis=0, tiled=True),
        lax.all_gather(key_weight, "ws", axis=0, tiled=True),
        lax.all_gather(value_weight, "ws", axis=0, tiled=True),
        lax.all_gather(output_weight, "ws", axis=0, tiled=True),
        lax.all_gather(gate_weight, "ws", axis=0, tiled=True),
        lax.all_gather(up_weight, "ws", axis=0, tiled=True),
        lax.all_gather(down_weight, "ws", axis=0, tiled=True),
        lax.all_gather(attn_gain, "ws", axis=0, tiled=True),
        lax.all_gather(ffn_gain, "ws", axis=0, tiled=True),
    )
    gain_attn = gain_first.astype(jnp.float32)
    gain_ffn = gain_second.astype(jnp.float32)
    inputs = tokens.astype(jnp.float32)
    first_pos = ctx_index * block_rows
    positions = (first_pos + jnp.arange(block_rows, dtype=jnp.int32)).astype(jnp.float32)
    cosine_table, sine_table = rope_tables(positions, HD)
    query_scale = 1.0 / math.sqrt(HD)
    normed = rms_scale(inputs, gain_attn).astype(jnp.bfloat16).reshape(-1, width)
    query_lin = jnp.dot(normed, full_query, preferred_element_type=jnp.float32)
    key_lin = jnp.dot(normed, full_key, preferred_element_type=jnp.float32)
    value_lin = jnp.dot(normed, full_value, preferred_element_type=jnp.float32)

    def turn_queries(linear):
        return (
            rotate_pairs(linear.reshape(seq_count, block_rows, H, HD), cosine_table, sine_table)
            * query_scale
        )

    def turn_keys(linear):
        return rotate_pairs(linear.reshape(seq_count, block_rows, KV, HD), cosine_table, sine_table)

    queries = turn_queries(query_lin).astype(jnp.bfloat16)
    queries = (
        queries.reshape(seq_count, block_rows, KV, groups, HD)
        .transpose(0, 2, 3, 1, 4)
        .reshape(seq_count, KV, group_rows, HD)
    )
    key_rows = turn_keys(key_lin).astype(jnp.bfloat16).reshape(seq_count, block_rows, kv_width)
    value_rows = value_lin.astype(jnp.bfloat16).reshape(seq_count, block_rows, kv_width)
    kv_own = jnp.concatenate([key_rows, value_rows], -1)
    query_pos = jnp.tile(first_pos + jnp.arange(block_rows, dtype=jnp.int32), groups)
    last_pos = first_pos + block_rows - 1

    def block_scores(kv_block, key_start):
        key_count = kv_block.shape[1]
        key_part = kv_block[..., :kv_width].reshape(seq_count, key_count, KV, HD)
        scores = jnp.einsum(
            "sard,skad->sark", queries, key_part, preferred_element_type=jnp.float32
        )
        key_pos = key_start + jnp.arange(key_count, dtype=jnp.int32)
        return jnp.where(query_pos[:, None] >= key_pos[None, :], scores, NEGATIVE)

    def each_block(update, carry, piece):
        piece_rows = piece.shape[1]
        step_rows = math.gcd(piece_rows, block_rows)

        def visit(block_index, state):
            key_start = block_index * step_rows
            kv_block = lax.dynamic_slice_in_dim(piece, block_index * step_rows, step_rows, 1)
            return lax.cond(
                key_start <= last_pos,
                lambda inner: update(inner, kv_block, key_start),
                lambda inner: inner,
                state,
            )

        return lax.fori_loop(0, piece_rows // step_rows, visit, carry)

    def add_stats(state, kv_block, key_start):
        run_max, run_sum = state
        scores = block_scores(kv_block, key_start)
        new_max = jnp.maximum(run_max, jnp.max(scores, -1))
        run_sum = run_sum * jnp.exp(run_max - new_max) + jnp.sum(
            jnp.exp(scores - new_max[..., None]), -1
        )
        return (new_max, run_sum)

    def add_values(total, kv_block, key_start):
        key_count = kv_block.shape[1]
        prob_low = jnp.exp(block_scores(kv_block, key_start) - log_total[..., None]).astype(
            jnp.bfloat16
        )
        value_part = kv_block[..., kv_width:].reshape(seq_count, key_count, KV, HD)
        return total + jnp.einsum(
            "sark,skad->sard", prob_low, value_part, preferred_element_type=jnp.float32
        )

    start_stats = (
        jnp.full((seq_count, KV, group_rows), NEGATIVE, jnp.float32),
        jnp.zeros((seq_count, KV, group_rows), jnp.float32),
    )
    start_values = jnp.zeros((seq_count, KV, group_rows, HD), jnp.float32)
    run_max, run_sum = each_block(
        add_stats, start_stats, lax.all_gather(kv_own, "ctx", axis=1, tiled=True)
    )
    log_total = run_max + jnp.log(run_sum)
    attended = each_block(
        add_values, start_values, lax.all_gather(kv_own, "ctx", axis=1, tiled=True)
    )
    attended_low = (
        attended.reshape(seq_count, KV, groups, block_rows, HD)
        .transpose(0, 3, 1, 2, 4)
        .reshape(-1, H * HD)
        .astype(jnp.bfloat16)
    )
    middle = inputs + jnp.dot(
        attended_low, full_output, preferred_element_type=jnp.float32
    ).reshape(seq_count, block_rows, width)
    normed_ffn = rms_scale(middle, gain_ffn).astype(jnp.bfloat16).reshape(-1, width)
    gate_rows = jnp.dot(normed_ffn, full_gate, preferred_element_type=jnp.float32)
    up_rows = jnp.dot(normed_ffn, full_up, preferred_element_type=jnp.float32)
    hidden = (jax.nn.silu(gate_rows) * up_rows).astype(jnp.bfloat16)
    result = middle + jnp.dot(hidden, full_down, preferred_element_type=jnp.float32).reshape(
        seq_count, block_rows, width
    )
    layer_out = result.astype(jnp.bfloat16)
    grad_rows = out_grad.reshape(-1, width)
    down_weight_grad = jnp.einsum(
        "nf,nd->fd", hidden, grad_rows, preferred_element_type=jnp.float32
    )
    hidden_grad = jnp.einsum("nd,fd->nf", grad_rows, full_down, preferred_element_type=jnp.float32)
    _, silu_pull = jax.vjp(lambda gate_in, up_in: jax.nn.silu(gate_in) * up_in, gate_rows, up_rows)
    gate_grad, up_grad = silu_pull(hidden_grad)
    gate_grad = gate_grad.astype(jnp.bfloat16)
    up_grad = up_grad.astype(jnp.bfloat16)
    gate_weight_grad = jnp.einsum(
        "nd,nf->df", normed_ffn, gate_grad, preferred_element_type=jnp.float32
    )
    up_weight_grad = jnp.einsum(
        "nd,nf->df", normed_ffn, up_grad, preferred_element_type=jnp.float32
    )
    normed_ffn_grad = jnp.einsum(
        "nf,df->nd", gate_grad, full_gate, preferred_element_type=jnp.float32
    )
    normed_ffn_grad = normed_ffn_grad + jnp.einsum(
        "nf,df->nd", up_grad, full_up, preferred_element_type=jnp.float32
    )
    _, ffn_pull = jax.vjp(rms_scale, middle, gain_ffn)
    middle_grad, ffn_gain_grad = ffn_pull(normed_ffn_grad.reshape(seq_count, block_rows, width))
    middle_grad = middle_grad + out_grad.astype(jnp.float32)
    branch_grad = middle_grad.reshape(-1, width).astype(jnp.bfloat16)
    output_weight_grad = jnp.einsum(
        "nh,nd->hd", attended_low, branch_grad, preferred_element_type=jnp.float32
    )
    attended_grad = jnp.einsum(
        "nd,hd->nh", branch_grad, full_output, preferred_element_type=jnp.float32
    ).astype(jnp.bfloat16)
    attended_grad = (
        attended_grad.reshape(seq_count, block_rows, KV, groups, HD)
        .transpose(0, 2, 3, 1, 4)
        .reshape(seq_count, KV, group_rows, HD)
    )
    row_delta = jnp.sum(attended_grad.astype(jnp.float32) * attended, -1)

    def backward_block(state, kv_block, key_start):
        query_grad, kv_grad = state
        prob = jnp.exp(block_scores(kv_block, key_start) - log_total[..., None])
        key_part = kv_block[..., :kv_width].reshape(seq_count, block_rows, KV, HD)
        value_part = kv_block[..., kv_width:].reshape(seq_count, block_rows, KV, HD)
        prob_grad = jnp.einsum(
            "sard,skad->sark", attended_grad, value_part, preferred_element_type=jnp.float32
        )
        score_grad = (prob * (prob_grad - row_delta[..., None])).astype(jnp.bfloat16)
        query_grad = query_grad + jnp.einsum(
            "sark,skad->sard", score_grad, key_part, preferred_element_type=jnp.float32
        )
        key_grad = jnp.einsum(
            "sark,sard->skad", score_grad, queries, preferred_element_type=jnp.float32
        ).reshape(seq_count, block_rows, kv_width)
        value_grad = jnp.einsum(
            "sark,sard->skad",
            prob.astype(jnp.bfloat16),
            attended_grad,
            preferred_element_type=jnp.float32,
        ).reshape(seq_count, block_rows, kv_width)
        return (query_grad, kv_grad + jnp.concatenate([key_grad, value_grad], -1))

    def cycle_step(step_index, state):
        kv_block, kv_grad, query_grad = state
        owner = (ctx_index - step_index) % ctx_count
        key_start = owner * block_rows
        current = kv_block
        query_grad, kv_grad = lax.cond(
            owner <= ctx_index,
            lambda inner: backward_block(inner, current, key_start),
            lambda inner: inner,
            (query_grad, kv_grad),
        )
        moved = from_behind(kv_block, "ctx", 1)
        kv_grad = passed_along(kv_grad.astype(jnp.bfloat16), "ctx", 1).astype(kv_grad.dtype)
        return (moved, kv_grad, query_grad)

    start_cycle = (
        kv_own,
        jnp.zeros((seq_count, block_rows, 2 * kv_width), jnp.float32),
        jnp.zeros((seq_count, KV, group_rows, HD), jnp.float32),
    )
    _, kv_grad, query_grad = lax.fori_loop(0, ctx_count, cycle_step, start_cycle)
    query_grad_rows = (
        query_grad.reshape(seq_count, KV, groups, block_rows, HD)
        .transpose(0, 3, 1, 2, 4)
        .reshape(seq_count, block_rows, H, HD)
    )
    _, query_pull = jax.vjp(turn_queries, query_lin)
    (query_lin_grad,) = query_pull(query_grad_rows)
    query_lin_grad = query_lin_grad.astype(jnp.bfloat16)
    _, key_pull = jax.vjp(turn_keys, key_lin)
    (key_lin_grad,) = key_pull(kv_grad[..., :kv_width].reshape(seq_count, block_rows, KV, HD))
    key_lin_grad = key_lin_grad.astype(jnp.bfloat16)
    value_lin_grad = kv_grad[..., kv_width:].reshape(-1, kv_width).astype(jnp.bfloat16)
    query_weight_grad = jnp.einsum(
        "nd,nh->dh", normed, query_lin_grad, preferred_element_type=jnp.float32
    )
    key_weight_grad = jnp.einsum(
        "nd,nh->dh", normed, key_lin_grad, preferred_element_type=jnp.float32
    )
    value_weight_grad = jnp.einsum(
        "nd,nh->dh", normed, value_lin_grad, preferred_element_type=jnp.float32
    )
    normed_grad = jnp.einsum(
        "nh,dh->nd", query_lin_grad, full_query, preferred_element_type=jnp.float32
    )
    normed_grad = normed_grad + jnp.einsum(
        "nh,dh->nd", key_lin_grad, full_key, preferred_element_type=jnp.float32
    )
    normed_grad = normed_grad + jnp.einsum(
        "nh,dh->nd", value_lin_grad, full_value, preferred_element_type=jnp.float32
    )
    _, attn_pull = jax.vjp(rms_scale, inputs, gain_attn)
    input_grad, attn_gain_grad = attn_pull(normed_grad.reshape(seq_count, block_rows, width))
    tokens_grad = (middle_grad + input_grad).astype(jnp.bfloat16)
    (
        share_attn,
        share_query,
        share_key,
        share_value,
        share_output,
        share_ffn,
        share_gate,
        share_up,
        share_down,
    ) = (
        lax.psum_scatter(
            attn_gain_grad.astype(jnp.bfloat16), "ws", scatter_dimension=0, tiled=True
        ).astype(jnp.float32),
        lax.psum_scatter(
            query_weight_grad.astype(jnp.bfloat16), "ws", scatter_dimension=0, tiled=True
        ).astype(jnp.float32),
        lax.psum_scatter(
            key_weight_grad.astype(jnp.bfloat16), "ws", scatter_dimension=0, tiled=True
        ).astype(jnp.float32),
        lax.psum_scatter(
            value_weight_grad.astype(jnp.bfloat16), "ws", scatter_dimension=0, tiled=True
        ).astype(jnp.float32),
        lax.psum_scatter(
            output_weight_grad.astype(jnp.bfloat16), "ws", scatter_dimension=0, tiled=True
        ).astype(jnp.float32),
        lax.psum_scatter(
            ffn_gain_grad.astype(jnp.bfloat16), "ws", scatter_dimension=0, tiled=True
        ).astype(jnp.float32),
        lax.psum_scatter(
            gate_weight_grad.astype(jnp.bfloat16), "ws", scatter_dimension=0, tiled=True
        ).astype(jnp.float32),
        lax.psum_scatter(
            up_weight_grad.astype(jnp.bfloat16), "ws", scatter_dimension=0, tiled=True
        ).astype(jnp.float32),
        lax.psum_scatter(
            down_weight_grad.astype(jnp.bfloat16), "ws", scatter_dimension=0, tiled=True
        ).astype(jnp.float32),
    )
    totals = lax.psum(
        (
            share_attn,
            share_query,
            share_key,
            share_value,
            share_output,
            share_ffn,
            share_gate,
            share_up,
            share_down,
        ),
        "ctx",
    )
    return (layer_out, tokens_grad) + tuple(totals)


def solution(mesh):
    in_specs = (
        P("ws", "ctx", None),
        P("ws"),
        P("ws", None),
        P("ws", None),
        P("ws", None),
        P("ws", None),
        P("ws"),
        P("ws", None),
        P("ws", None),
        P("ws", None),
        P("ws", "ctx", None),
    )
    out_specs = (
        P("ws", "ctx", None),
        P("ws", "ctx", None),
        P("ws"),
        P("ws", None),
        P("ws", None),
        P("ws", None),
        P("ws", None),
        P("ws"),
        P("ws", None),
        P("ws", None),
        P("ws", None),
    )
    return jax.shard_map(body, mesh=mesh, in_specs=in_specs, out_specs=out_specs, check_vma=False)
```

profile of v0, /device:TPU:0, one launch (start us, length us, event | category | flops | bytes accessed | tf_op | source)
XLA Modules:
  0.0 649.2 jit_solution(8871774034944697349)
XLA Ops:
  7.3 1.4 fusion.88
  11.0 8.3 %all-reduce.10 = (bf16[576]{0:T(1024)(128)(2,1)S(1)}, bf16[576]{0:T(1024)(128)(2,1)S(1)}) all-reduce(bf16[576]{0:T(1024)(128)(2,1)S(1)} %dynamic-update-slice, bf16[576]{0:T(1024)(128)(2,1)S(1)} %dynamic-update-slice.1), channel_id=1, replica_groups=mesh['ctx'=8,'ws'=4] {'ws'}, use_global_device_ids=true, to_apply=%add.4 | all-reduce | flops 1152 | bytes 4608
  20.4 6.1 all_gather.32
  27.2 1.4 fusion.83
  29.5 6.0 all_gather.33
  39.6 8.4 %all_gather.35 = bf16[576,576]{1,0:T(8,128)(2,1)S(1)} all-gather(bf16[144,576]{1,0:T(8,128)(2,1)S(1)} %copy-done.39), channel_id=1, replica_groups=mesh['ctx'=8,'ws'=4] {'ws'}, dimensions={0}, use_global_device_ids=true | all-gather | bytes 829440 | tf_op jit(solution)/shard_map/all_gather | solution.py:80
  49.5 8.6 %all_gather.36 = bf16[576,576]{1,0:T(8,128)(2,1)S(1)} all-gather(bf16[144,576]{1,0:T(8,128)(2,1)S(1)} %copy-done.40), channel_id=1, replica_groups=mesh['ctx'=8,'ws'=4] {'ws'}, dimensions={0}, use_global_device_ids=true | all-gather | bytes 829440 | tf_op jit(solution)/shard_map/all_gather | solution.py:83
  58.2 25.1 %all-gather.5.cloned.1.call-done = bf16[1,2048,384]{1,2,0:T(8,128)(2,1)} async-done(((bf16[1,256,384]{1,2,0:T(8,128)(2,1)}), bf16[1,2048,384]{1,2,0:T(8,128)(2,1)}) %all-gather.5.cloned.1.call-update) | async-done | bytes 1572880 | tf_op jit(solution)/shard_map/all_gather | solution.py:177
  83.3 2.5 while.53
  83.3 2.2 conditional.9
  85.9 2.4 while.54
  85.9 2.1 conditional.10
  90.0 13.8 %all-gather.7.cloned.1.call-done = bf16[576,1536]{1,0:T(8,128)(2,1)} async-done(((bf16[144,1536]{1,0:T(8,128)(2,1)}), bf16[576,1536]{1,0:T(8,128)(2,1)}) %all-gather.7.cloned.1.call-update) | async-done | bytes 1769488 | tf_op jit(solution)/shard_map/all_gather | solution.py:84
  103.8 3.4 fusion.89
  107.2 19.0 %all-gather.9.cloned.1.call-done = bf16[576,1536]{1,0:T(8,128)(2,1)} async-done(((bf16[144,1536]{1,0:T(8,128)(2,1)}), bf16[576,1536]{1,0:T(8,128)(2,1)}) %all-gather.9.cloned.1.call-update) | async-done | bytes 1769488 | tf_op jit(solution)/shard_map/all_gather | solution.py:85
  126.2 3.5 fusion.90
  129.7 18.7 %all-gather.11.cloned.1.call-done = bf16[1536,576]{0,1:T(8,128)(2,1)} async-done(((bf16[384,576]{0,1:T(8,128)(2,1)}), bf16[1536,576]{0,1:T(8,128)(2,1)}) %all-gather.11.cloned.1.call-update) | async-done | bytes 1769488 | tf_op jit(solution)/shard_map/all_gather | solution.py:86
  148.4 4.7 multiply_convert_fusion.1
  153.8 1.4 copy-done.10
  155.2 1.4 fusion.55
  159.4 1.6 multiply_reduce_fusion
  161.9 134.6 %while.55 = (s32[]{:T(128)}, bf16[1,256,384]{1,2,0:T(8,128)(2,1)S(1)}, f32[1,256,384]{1,2,0:T(8,128)S(1)}, f32[1,3,768,64]{2,3,1,0:T(8,128)}, s32[]{:T(128)}, /*...) while((s32[]{:T(128)}, ...), condition=%wide.region_17.18_spmd.clone, body=%wide.region_14.17_spmd.clone.sunk | while | flops 383041792 | bytes 19876380 | solution.py:277
  162.0 7.3 %conditional.11 = ((f32[1,3,768,64]{2,3,1,0:T(8,128)}, f32[1,256,384]{1,2,0:T(8,128)S(1)})) conditional(s32[]{:T(128)} %convert_element_type.393, (f32[1,3,768,64]{2,3,1,0:T(8,128)}, f32[1,256,384]{1,2,0:T(8,128)S(1)}) %tuple.173, (s32[256]{0:T(256)S(1)}, s32[]{:T(128)}, bf16[1,3,768,64]{2,3,1,0:T(8,128)(2,1)S(1)}, ...), branch_computations={%region_15.15_spmd, %region_16.16_spmd} | conditional | flops 382746880 | bytes 15943776 | solution.py:262
  162.8 2.0 multiply_convert_fusion
  165.1 1.6 fusion.23
  166.9 2.4 fusion.22
  169.3 1.5 collective-permute-start.1
  170.8 3.4 collective-permute-start
  174.2 4.9 collective-permute-done.1
  179.7 9.8 %collective-permute-start.1 = (bf16[1,256,384]{1,2,0:T(8,128)(2,1)S(1)}, bf16[1,256,384]{1,2,0:T(8,128)(2,1)S(1)}, u32[]{:S(2)}, u32[]{:S(2)}) collective-permute-start(bf16[1,256,384]{1,2,0:T(8,128)(2,1)S(1)} %convert_element_type.394), channel_id=1, source_target_pairs={{0,4},{4,8},{8,12},{12,16},{16,20},{20,24},{24,28},{28,0},{1,5},{5... | collective-permute-start | bytes 589832 | tf_op jit(solution)/shard_map/while/body/eval_jaxpr/ppermute | solution.py:27
  189.5 4.3 collective-permute-start
  193.8 3.0 collective-permute-done.1
  197.6 2.5 collective-permute-start.1
  200.1 12.5 %collective-permute-start = (bf16[1,256,384]{1,2,0:T(8,128)(2,1)S(1)}, bf16[1,256,384]{1,2,0:T(8,128)(2,1)S(1)}, u32[]{:S(2)}, u32[]{:S(2)}) collective-permute-start(bf16[1,256,384]{1,2,0:T(8,128)(2,1)S(1)} %copy.80), channel_id=1, source_target_pairs={{0,4},{4,8},{8,12},{12,16},{16,20},{20,24},{24,28},{1,5},{5,9},{9,... | collective-permute-start | bytes 589832 | tf_op jit(solution)/shard_map/while/body/eval_jaxpr/ppermute | solution.py:21
  213.8 1.9 collective-permute-done
  215.9 2.6 collective-permute-start.1
  218.5 4.7 collective-permute-start
  223.2 8.2 %collective-permute-done.1 = bf16[1,256,384]{1,2,0:T(8,128)(2,1)S(1)} collective-permute-done((bf16[1,256,384]{1,2,0:T(8,128)(2,1)S(1)}, bf16[1,256,384]{1,2,0:T(8,128)(2,1)S(1)}, u32[]{:S(2)}, u32[]{:S(2)}) %collective-permute-start.1) | collective-permute-done | bytes 196640 | tf_op jit(solution)/shard_map/while/body/eval_jaxpr/ppermute | solution.py:27
  231.6 2.2 collective-permute-start.1
  233.9 5.3 collective-permute-start
  239.2 9.2 %collective-permute-done.1 = bf16[1,256,384]{1,2,0:T(8,128)(2,1)S(1)} collective-permute-done((bf16[1,256,384]{1,2,0:T(8,128)(2,1)S(1)}, bf16[1,256,384]{1,2,0:T(8,128)(2,1)S(1)}, u32[]{:S(2)}, u32[]{:S(2)}) %collective-permute-start.1) | collective-permute-done | bytes 196640 | tf_op jit(solution)/shard_map/while/body/eval_jaxpr/ppermute | solution.py:27
  248.7 8.5 %collective-permute-start = (bf16[1,256,384]{1,2,0:T(8,128)(2,1)S(1)}, bf16[1,256,384]{1,2,0:T(8,128)(2,1)S(1)}, u32[]{:S(2)}, u32[]{:S(2)}) collective-permute-start(bf16[1,256,384]{1,2,0:T(8,128)(2,1)S(1)} %copy.80), channel_id=1, source_target_pairs={{0,4},{4,8},{8,12},{12,16},{16,20},{20,24},{24,28},{1,5},{5,9},{9,... | collective-permute-start | bytes 589832 | tf_op jit(solution)/shard_map/while/body/eval_jaxpr/ppermute | solution.py:21
  257.2 7.2 %collective-permute-done.1 = bf16[1,256,384]{1,2,0:T(8,128)(2,1)S(1)} collective-permute-done((bf16[1,256,384]{1,2,0:T(8,128)(2,1)S(1)}, bf16[1,256,384]{1,2,0:T(8,128)(2,1)S(1)}, u32[]{:S(2)}, u32[]{:S(2)}) %collective-permute-start.1) | collective-permute-done | bytes 196640 | tf_op jit(solution)/shard_map/while/body/eval_jaxpr/ppermute | solution.py:27
  264.7 4.4 collective-permute-start
  269.1 11.3 %collective-permute-done.1 = bf16[1,256,384]{1,2,0:T(8,128)(2,1)S(1)} collective-permute-done((bf16[1,256,384]{1,2,0:T(8,128)(2,1)S(1)}, bf16[1,256,384]{1,2,0:T(8,128)(2,1)S(1)}, u32[]{:S(2)}, u32[]{:S(2)}) %collective-permute-start.1) | collective-permute-done | bytes 196640 | tf_op jit(solution)/shard_map/while/body/eval_jaxpr/ppermute | solution.py:27
  280.6 4.2 collective-permute-start
  284.8 11.7 %collective-permute-done.1 = bf16[1,256,384]{1,2,0:T(8,128)(2,1)S(1)} collective-permute-done((bf16[1,256,384]{1,2,0:T(8,128)(2,1)S(1)}, bf16[1,256,384]{1,2,0:T(8,128)(2,1)S(1)}, u32[]{:S(2)}, u32[]{:S(2)}) %collective-permute-start.1) | collective-permute-done | bytes 196640 | tf_op jit(solution)/shard_map/while/body/eval_jaxpr/ppermute | solution.py:27
  296.6 1.4 reshape.532
  302.3 1.4 convolution_convert_fusion.4
  303.8 1.3 convolution_convert_fusion.3
  305.2 1.9 convolution_convert_fusion
  307.1 3.9 copy.43
  311.9 3.0 convolution_convert_fusion.2
  315.0 3.0 convolution_convert_fusion.1
  320.3 5.9 all-reduce.9
  327.8 1.4 fusion.41
  329.2 15.1 %reduce-scatter.14.cloned.1.call-done = bf16[144,192]{1,0:T(8,128)(2,1)} async-done(((bf16[576,192]{1,0:T(8,128)(2,1)}), bf16[144,192]{1,0:T(8,128)(2,1)}) %reduce-scatter.14.cloned.1.call-update) | async-done | bytes 55312 | tf_op jit(solution)/shard_map/reduce_scatter | solution.py:331
  344.2 25.5 %reduce-scatter.10.cloned.1.call-done = bf16[144,576]{1,0:T(8,128)(2,1)} async-done(((bf16[576,576]{1,0:T(8,128)(2,1)}), bf16[144,576]{1,0:T(8,128)(2,1)}) %reduce-scatter.10.cloned.1.call-update) | async-done | bytes 165904 | tf_op jit(solution)/shard_map/reduce_scatter | solution.py:325
  369.8 25.7 %reduce-scatter.16.cloned.1.call-done = bf16[144,576]{1,0:T(8,128)(2,1)} async-done(((bf16[576,576]{1,0:T(8,128)(2,1)}), bf16[144,576]{1,0:T(8,128)(2,1)}) %reduce-scatter.16.cloned.1.call-update) | async-done | bytes 165904 | tf_op jit(solution)/shard_map/reduce_scatter | solution.py:334
  395.4 33.2 %reduce-scatter.22.cloned.1.call-done = bf16[384,576]{1,0:T(8,128)(2,1)} async-done(((bf16[1536,576]{1,0:T(8,128)(2,1)}), bf16[384,576]{1,0:T(8,128)(2,1)}) %reduce-scatter.22.cloned.1.call-update) | async-done | bytes 442384
  428.7 1.3 copy.44
  429.9 30.7 %reduce-scatter.18.cloned.1.call-done = bf16[144,1536]{1,0:T(8,128)(2,1)} async-done(((bf16[576,1536]{1,0:T(8,128)(2,1)}), bf16[144,1536]{1,0:T(8,128)(2,1)}) %reduce-scatter.18.cloned.1.call-update) | async-done | bytes 442384 | tf_op jit(solution)/shard_map/reduce_scatter | solution.py:340
  460.7 32.0 %reduce-scatter.20.cloned.1.call-done = bf16[144,1536]{1,0:T(8,128)(2,1)} async-done(((bf16[576,1536]{1,0:T(8,128)(2,1)}), bf16[144,1536]{1,0:T(8,128)(2,1)}) %reduce-scatter.20.cloned.1.call-update) | async-done | bytes 442384 | tf_op jit(solution)/shard_map/reduce_scatter | solution.py:343
  492.7 150.0 %all-reduce.12 = (f32[144]{0:T(256)}, f32[144,576]{1,0:T(8,128)}, f32[144,192]{1,0:T(8,128)}, f32[144,192]{1,0:T(8,128)}, f32[144,576]{1,0:T(8,128)}, /*index=5*...) all-reduce(f32[144]{0:T(256)S(1)} %get-tuple-element.897, ...), channel_id=1, replica_groups=mesh['ctx'=8,'ws'=4] {'ctx'}, use_global_device_ids=true, to_apply=%region_21.22 | all-reduce | flops 885024 | bytes 5310720 | tf_op jit(solution)/shard_map/psum | solution.py:350
  (258 shorter events, 33.2 us)
Async XLA Ops:
  7.2 29.1 %copy-start.2 = (bf16[1,256,576]{1,2,0:T(8,128)(2,1)S(1)}, bf16[1,256,576]{1,2,0:T(8,128)(2,1)}, u32[]{:S(2)}) copy-start(bf16[1,256,576]{1,2,0:T(8,128)(2,1)} %param.23) | copy-start | bytes 884740
  7.2 22.3 %copy-start.41 = (bf16[144,192]{1,0:T(8,128)(2,1)S(1)}, bf16[144,192]{1,0:T(8,128)(2,1)}, u32[]{:S(2)}) copy-start(bf16[144,192]{1,0:T(8,128)(2,1)} %param.27) | copy-start | bytes 165892
  7.2 76.1 %all-gather.5.cloned.1.call-start = ((), (), s32[]{:S(2)}) async-start(), calls=%async_computation.7 | async-start | bytes 1769472 | tf_op jit(solution)/shard_map/all_gather | solution.py:177
  29.5 19.2 %copy-start.31 = (f32[256,64]{0,1:T(8,128)}, f32[256,64]{0,1:T(8,128)S(1)}, u32[]{:S(2)}) copy-start(f32[256,64]{0,1:T(8,128)S(1)} %get-tuple-element.889) | copy-start | bytes 196612
  29.5 19.2 %copy-start.33 = (f32[256,64]{0,1:T(8,128)}, f32[256,64]{0,1:T(8,128)S(1)}, u32[]{:S(2)}) copy-start(f32[256,64]{0,1:T(8,128)S(1)} %get-tuple-element.888) | copy-start | bytes 196612
  36.2 3.3 copy-start.39
  37.4 66.4 %all-gather.7.cloned.1.call-start = ((), (), s32[]{:S(2)}) async-start(), calls=%async_computation.8 | async-start | bytes 2211840 | tf_op jit(solution)/shard_map/all_gather | solution.py:84
  38.2 88.0 %all-gather.9.cloned.1.call-start = ((), (), s32[]{:S(2)}) async-start(), calls=%async_computation.9 | async-start | bytes 2211840 | tf_op jit(solution)/shard_map/all_gather | solution.py:85
  38.9 109.4 %all-gather.11.cloned.1.call-start = ((), (), s32[]{:S(2)}) async-start(), calls=%async_computation.10 | async-start | bytes 2211840 | tf_op jit(solution)/shard_map/all_gather | solution.py:86
  39.5 289.7 %reduce-scatter.12.cloned.1.call-start = ((), (), s32[]{:S(2)}) async-start(), calls=%async_computation.12 | async-start | bytes 368640 | tf_op jit(solution)/shard_map/reduce_scatter | solution.py:328
  48.6 0.9 copy-start.40
  58.2 30.9 %copy-start.13 = (bf16[576,576]{1,0:T(8,128)(2,1)}, bf16[576,576]{1,0:T(8,128)(2,1)S(1)}, u32[]{:S(2)}) copy-start(bf16[576,576]{1,0:T(8,128)(2,1)S(1)} %all_gather.36) | copy-start | bytes 1990660
  88.3 1.3 copy-start.43
  89.6 66.9 %copy-start = (f32[1,256,576]{1,2,0:T(8,128)}, f32[1,256,576]{1,2,0:T(8,128)S(1)}, u32[]{:S(2)}) copy-start(f32[1,256,576]{1,2,0:T(8,128)S(1)} %get-tuple-element.893) | copy-start | bytes 1769476
  90.0 36.2 %copy-start.7 = (bf16[256,576]{0,1:T(8,128)(2,1)}, bf16[256,576]{0,1:T(8,128)(2,1)S(1)}, u32[]{:S(2)}) copy-start(bf16[256,576]{0,1:T(8,128)(2,1)S(1)} %fusion.57) | copy-start | bytes 884740
  129.7 23.4 %copy-start.9 = (bf16[576,1536]{1,0:T(8,128)(2,1)S(1)}, bf16[576,1536]{1,0:T(8,128)(2,1)}, u32[]{:S(2)}) copy-start(bf16[576,1536]{1,0:T(8,128)(2,1)} %all-gather.7.cloned.1.call-done) | copy-start | bytes 5308420
  153.1 3.4 copy-start.19
  153.1 4.9 copy-start.18
  153.1 2.0 copy-start.10
  155.2 1.4 copy-start.25
  156.5 1.1 copy-start.14
  156.7 0.9 copy-start.5
  157.6 1.7 copy-start.16
  158.0 3.9 copy-start.4
  169.3 9.8 %collective-permute-start.1 = (bf16[1,256,384]{1,2,0:T(8,128)(2,1)S(1)}, bf16[1,256,384]{1,2,0:T(8,128)(2,1)S(1)}, u32[]{:S(2)}, u32[]{:S(2)}) collective-permute-start(bf16[1,256,384]{1,2,0:T(8,128)(2,1)S(1)} %convert_element_type.394), channel_id=1, source_target_pairs={{0,4},{4,8},{8,12},{12,16},{16,20},{20,24},{24,28},{28,0},{1,5},{5... | collective-permute-start | bytes 589832 | tf_op jit(solution)/shard_map/while/body/eval_jaxpr/ppermute | solution.py:27
  170.8 8.8 %collective-permute-start = (bf16[1,256,384]{1,2,0:T(8,128)(2,1)S(1)}, bf16[1,256,384]{1,2,0:T(8,128)(2,1)S(1)}, u32[]{:S(2)}, u32[]{:S(2)}) collective-permute-start(bf16[1,256,384]{1,2,0:T(8,128)(2,1)S(1)} %copy.80), channel_id=1, source_target_pairs={{0,4},{4,8},{8,12},{12,16},{16,20},{20,24},{24,28},{1,5},{5,9},{9,... | collective-permute-start | bytes 589832 | tf_op jit(solution)/shard_map/while/body/eval_jaxpr/ppermute | solution.py:21
  179.7 17.0 %collective-permute-start.1 = (bf16[1,256,384]{1,2,0:T(8,128)(2,1)S(1)}, bf16[1,256,384]{1,2,0:T(8,128)(2,1)S(1)}, u32[]{:S(2)}, u32[]{:S(2)}) collective-permute-start(bf16[1,256,384]{1,2,0:T(8,128)(2,1)S(1)} %convert_element_type.394), channel_id=1, source_target_pairs={{0,4},{4,8},{8,12},{12,16},{16,20},{20,24},{24,28},{28,0},{1,5},{5... | collective-permute-start | bytes 589832 | tf_op jit(solution)/shard_map/while/body/eval_jaxpr/ppermute | solution.py:27
  189.5 7.9 %collective-permute-start = (bf16[1,256,384]{1,2,0:T(8,128)(2,1)S(1)}, bf16[1,256,384]{1,2,0:T(8,128)(2,1)S(1)}, u32[]{:S(2)}, u32[]{:S(2)}) collective-permute-start(bf16[1,256,384]{1,2,0:T(8,128)(2,1)S(1)} %copy.80), channel_id=1, source_target_pairs={{0,4},{4,8},{8,12},{12,16},{16,20},{20,24},{24,28},{1,5},{5,9},{9,... | collective-permute-start | bytes 589832 | tf_op jit(solution)/shard_map/while/body/eval_jaxpr/ppermute | solution.py:21
  197.6 16.2 %collective-permute-start.1 = (bf16[1,256,384]{1,2,0:T(8,128)(2,1)S(1)}, bf16[1,256,384]{1,2,0:T(8,128)(2,1)S(1)}, u32[]{:S(2)}, u32[]{:S(2)}) collective-permute-start(bf16[1,256,384]{1,2,0:T(8,128)(2,1)S(1)} %convert_element_type.394), channel_id=1, source_target_pairs={{0,4},{4,8},{8,12},{12,16},{16,20},{20,24},{24,28},{28,0},{1,5},{5... | collective-permute-start | bytes 589832 | tf_op jit(solution)/shard_map/while/body/eval_jaxpr/ppermute | solution.py:27
  200.1 15.6 %collective-permute-start = (bf16[1,256,384]{1,2,0:T(8,128)(2,1)S(1)}, bf16[1,256,384]{1,2,0:T(8,128)(2,1)S(1)}, u32[]{:S(2)}, u32[]{:S(2)}) collective-permute-start(bf16[1,256,384]{1,2,0:T(8,128)(2,1)S(1)} %copy.80), channel_id=1, source_target_pairs={{0,4},{4,8},{8,12},{12,16},{16,20},{20,24},{24,28},{1,5},{5,9},{9,... | collective-permute-start | bytes 589832 | tf_op jit(solution)/shard_map/while/body/eval_jaxpr/ppermute | solution.py:21
  215.9 15.6 %collective-permute-start.1 = (bf16[1,256,384]{1,2,0:T(8,128)(2,1)S(1)}, bf16[1,256,384]{1,2,0:T(8,128)(2,1)S(1)}, u32[]{:S(2)}, u32[]{:S(2)}) collective-permute-start(bf16[1,256,384]{1,2,0:T(8,128)(2,1)S(1)} %convert_element_type.394), channel_id=1, source_target_pairs={{0,4},{4,8},{8,12},{12,16},{16,20},{20,24},{24,28},{28,0},{1,5},{5... | collective-permute-start | bytes 589832 | tf_op jit(solution)/shard_map/while/body/eval_jaxpr/ppermute | solution.py:27
  218.5 13.0 %collective-permute-start = (bf16[1,256,384]{1,2,0:T(8,128)(2,1)S(1)}, bf16[1,256,384]{1,2,0:T(8,128)(2,1)S(1)}, u32[]{:S(2)}, u32[]{:S(2)}) collective-permute-start(bf16[1,256,384]{1,2,0:T(8,128)(2,1)S(1)} %copy.80), channel_id=1, source_target_pairs={{0,4},{4,8},{8,12},{12,16},{16,20},{20,24},{24,28},{1,5},{5,9},{9,... | collective-permute-start | bytes 589832 | tf_op jit(solution)/shard_map/while/body/eval_jaxpr/ppermute | solution.py:21
  231.6 16.7 %collective-permute-start.1 = (bf16[1,256,384]{1,2,0:T(8,128)(2,1)S(1)}, bf16[1,256,384]{1,2,0:T(8,128)(2,1)S(1)}, u32[]{:S(2)}, u32[]{:S(2)}) collective-permute-start(bf16[1,256,384]{1,2,0:T(8,128)(2,1)S(1)} %convert_element_type.394), channel_id=1, source_target_pairs={{0,4},{4,8},{8,12},{12,16},{16,20},{20,24},{24,28},{28,0},{1,5},{5... | collective-permute-start | bytes 589832 | tf_op jit(solution)/shard_map/while/body/eval_jaxpr/ppermute | solution.py:27
  233.9 14.6 %collective-permute-start = (bf16[1,256,384]{1,2,0:T(8,128)(2,1)S(1)}, bf16[1,256,384]{1,2,0:T(8,128)(2,1)S(1)}, u32[]{:S(2)}, u32[]{:S(2)}) collective-permute-start(bf16[1,256,384]{1,2,0:T(8,128)(2,1)S(1)} %copy.80), channel_id=1, source_target_pairs={{0,4},{4,8},{8,12},{12,16},{16,20},{20,24},{24,28},{1,5},{5,9},{9,... | collective-permute-start | bytes 589832 | tf_op jit(solution)/shard_map/while/body/eval_jaxpr/ppermute | solution.py:21
  248.6 15.8 %collective-permute-start.1 = (bf16[1,256,384]{1,2,0:T(8,128)(2,1)S(1)}, bf16[1,256,384]{1,2,0:T(8,128)(2,1)S(1)}, u32[]{:S(2)}, u32[]{:S(2)}) collective-permute-start(bf16[1,256,384]{1,2,0:T(8,128)(2,1)S(1)} %convert_element_type.394), channel_id=1, source_target_pairs={{0,4},{4,8},{8,12},{12,16},{16,20},{20,24},{24,28},{28,0},{1,5},{5... | collective-permute-start | bytes 589832 | tf_op jit(solution)/shard_map/while/body/eval_jaxpr/ppermute | solution.py:27
  248.7 15.8 %collective-permute-start = (bf16[1,256,384]{1,2,0:T(8,128)(2,1)S(1)}, bf16[1,256,384]{1,2,0:T(8,128)(2,1)S(1)}, u32[]{:S(2)}, u32[]{:S(2)}) collective-permute-start(bf16[1,256,384]{1,2,0:T(8,128)(2,1)S(1)} %copy.80), channel_id=1, source_target_pairs={{0,4},{4,8},{8,12},{12,16},{16,20},{20,24},{24,28},{1,5},{5,9},{9,... | collective-permute-start | bytes 589832 | tf_op jit(solution)/shard_map/while/body/eval_jaxpr/ppermute | solution.py:21
  264.6 15.7 %collective-permute-start.1 = (bf16[1,256,384]{1,2,0:T(8,128)(2,1)S(1)}, bf16[1,256,384]{1,2,0:T(8,128)(2,1)S(1)}, u32[]{:S(2)}, u32[]{:S(2)}) collective-permute-start(bf16[1,256,384]{1,2,0:T(8,128)(2,1)S(1)} %convert_element_type.394), channel_id=1, source_target_pairs={{0,4},{4,8},{8,12},{12,16},{16,20},{20,24},{24,28},{28,0},{1,5},{5... | collective-permute-start | bytes 589832 | tf_op jit(solution)/shard_map/while/body/eval_jaxpr/ppermute | solution.py:27
  264.7 15.7 %collective-permute-start = (bf16[1,256,384]{1,2,0:T(8,128)(2,1)S(1)}, bf16[1,256,384]{1,2,0:T(8,128)(2,1)S(1)}, u32[]{:S(2)}, u32[]{:S(2)}) collective-permute-start(bf16[1,256,384]{1,2,0:T(8,128)(2,1)S(1)} %copy.80), channel_id=1, source_target_pairs={{0,4},{4,8},{8,12},{12,16},{16,20},{20,24},{24,28},{1,5},{5,9},{9,... | collective-permute-start | bytes 589832 | tf_op jit(solution)/shard_map/while/body/eval_jaxpr/ppermute | solution.py:21
  280.5 15.9 %collective-permute-start.1 = (bf16[1,256,384]{1,2,0:T(8,128)(2,1)S(1)}, bf16[1,256,384]{1,2,0:T(8,128)(2,1)S(1)}, u32[]{:S(2)}, u32[]{:S(2)}) collective-permute-start(bf16[1,256,384]{1,2,0:T(8,128)(2,1)S(1)} %convert_element_type.394), channel_id=1, source_target_pairs={{0,4},{4,8},{8,12},{12,16},{16,20},{20,24},{24,28},{28,0},{1,5},{5... | collective-permute-start | bytes 589832 | tf_op jit(solution)/shard_map/while/body/eval_jaxpr/ppermute | solution.py:27
  280.6 15.9 %collective-permute-start = (bf16[1,256,384]{1,2,0:T(8,128)(2,1)S(1)}, bf16[1,256,384]{1,2,0:T(8,128)(2,1)S(1)}, u32[]{:S(2)}, u32[]{:S(2)}) collective-permute-start(bf16[1,256,384]{1,2,0:T(8,128)(2,1)S(1)} %copy.80), channel_id=1, source_target_pairs={{0,4},{4,8},{8,12},{12,16},{16,20},{20,24},{24,28},{1,5},{5,9},{9,... | collective-permute-start | bytes 589832 | tf_op jit(solution)/shard_map/while/body/eval_jaxpr/ppermute | solution.py:21
  296.5 1.6 copy-start.34
  296.6 1.6 copy-start.32
  298.0 1.0 copy-start.3
  298.1 1.9 copy-start.38
  300.0 1.5 copy-start.37
  300.0 44.3 %reduce-scatter.14.cloned.1.call-start = ((), (), s32[]{:S(2)}) async-start(), calls=%async_computation.13 | async-start | bytes 368640 | tf_op jit(solution)/shard_map/reduce_scatter | solution.py:331
  301.2 68.6 %reduce-scatter.10.cloned.1.call-start = ((), (), s32[]{:S(2)}) async-start(), calls=%async_computation.11 | async-start | bytes 921600 | tf_op jit(solution)/shard_map/reduce_scatter | solution.py:325
  301.4 2.3 copy-start.6
  301.5 2.3 copy-start.21
  303.7 1.5 copy-start.17
  303.7 1.5 copy-start.26
  303.7 91.7 %reduce-scatter.16.cloned.1.call-start = ((), (), s32[]{:S(2)}) async-start(), calls=%async_computation.14 | async-start | bytes 921600 | tf_op jit(solution)/shard_map/reduce_scatter | solution.py:334
  305.1 123.6 %reduce-scatter.22.cloned.1.call-start = ((), (), s32[]{:S(2)}) async-start(), calls=%async_computation.17 | async-start | bytes 2457600
  311.0 1.0 copy-start.8
  311.0 149.7 %reduce-scatter.18.cloned.1.call-start = ((), (), s32[]{:S(2)}) async-start(), calls=%async_computation.15 | async-start | bytes 2211840 | tf_op jit(solution)/shard_map/reduce_scatter | solution.py:340
  314.9 3.8 copy-start.28
  315.0 3.8 copy-start.36
  315.0 177.7 %reduce-scatter.20.cloned.1.call-start = ((), (), s32[]{:S(2)}) async-start(), calls=%async_computation.16 | async-start | bytes 2211840 | tf_op jit(solution)/shard_map/reduce_scatter | solution.py:343
  318.0 1.1 copy-start.12
  318.0 1.2 copy-start.23
  318.8 1.0 copy-start.30
  319.2 1.0 copy-start.45
  319.8 7.4 %copy-start.1 = (f32[1,256,576]{1,2,0:T(8,128)S(1)}, f32[1,256,576]{1,2,0:T(8,128)}, u32[]{:S(2)}) copy-start(f32[1,256,576]{1,2,0:T(8,128)} %copy-done) | copy-start | bytes 1769476
  326.2 1.6 copy-start.24
  (9 other events, 6.8 us)
Sparse Core Ops, SparseCore 0:
  37.6 45.6 all-gather.4
  84.8 18.9 all-gather.6
  105.4 20.7 all-gather.8
  127.6 20.7 all-gather.10
  300.1 21.3 reduce-scatter.11
  323.9 20.2 reduce-scatter.13
  346.8 22.9 reduce-scatter.9
  372.5 22.9 reduce-scatter.15
  398.0 30.6 reduce-scatter.21
  431.3 29.3 reduce-scatter.17
  463.3 29.3 reduce-scatter.19
where the time goes:
time: 652 us; the launch traced here: 649 us
  waiting for transfers between devices  301 us (46%)
  blocking collectives  193 us (30%)
  starting transfers between devices  66.7 us (10%)
  matrix products  40.3 us (6%)
  local copies, waits for them, and re-layouts  22.8 us (3%)
  between operations  15.9 us (2%)
  other arithmetic  7.94 us (1%)
    psum x1, blocking collectives, body(): lax.psum((share_attn, share_query, share_key, share_value, share_output,...  150 us
    ppermute x8, waiting for transfers between devices, passed_along(): return lax.ppermute(value, axis, pairs)  56.7 us
    ppermute x8, starting transfers between devices, from_behind(): return lax.ppermute(array, axis, pairs)  47.1 us
    unnamed x12, waiting for transfers between devices  35.3 us
    reduce_scatter x1, waiting for transfers between devices, body(): lax.psum_scatter(up_weight_grad.astype(jnp.bfloat16), 'ws', scatter_dimen...  32 us
    reduce_scatter x1, waiting for transfers between devices, body(): lax.psum_scatter(gate_weight_grad.astype(jnp.bfloat16), 'ws', scatter_dim...  30.7 us
    reduce_scatter x1, waiting for transfers between devices, body(): lax.psum_scatter(output_weight_grad.astype(jnp.bfloat16), 'ws', scatter_d...  25.7 us
    reduce_scatter x1, waiting for transfers between devices, body(): lax.psum_scatter(query_weight_grad.astype(jnp.bfloat16), 'ws', scatter_di...  25.5 us
  transfers between devices with their start and end apart: 27, of which 21 were waited for; matrix products, arithmetic and copies ran while one was open for 5% of the time, Pallas kernels for 0%

commit v1 on v0

v1 whole, which is shorter than its diff:
```python
import functools
import math

import jax
import jax.numpy as jnp
from jax import lax
from jax.experimental import pallas as pl
from jax.experimental.pallas import tpu as pltpu
from jax.sharding import PartitionSpec as P

H = 9
KV = 3
HD = 64
GROUPS = H // KV
KVW = KV * HD

EPS = 1e-05
THETA = 100000.0
NEGATIVE = -1e30
LANES = 128
FF_STEP = 256
VMEM_LIMIT = 60 * 1024 * 1024

BF16 = jnp.bfloat16
F32 = jnp.float32

SMEM_SPEC = pl.BlockSpec(memory_space=pltpu.SMEM)
VMEM_SPEC = pl.BlockSpec(memory_space=pltpu.VMEM)


def mm(left, right, left_dim=1, right_dim=0):
    return lax.dot_general(
        left, right, (((left_dim,), (right_dim,)), ((), ())), preferred_element_type=F32
    )


def call(kernel, outs, args, scratch=(), flops=0, moved=0, smem=0):
    return pl.pallas_call(
        kernel,
        out_shape=outs,
        in_specs=[SMEM_SPEC] * smem + [VMEM_SPEC] * (len(args) - smem),
        out_specs=jax.tree.map(lambda _: VMEM_SPEC, outs),
        scratch_shapes=list(scratch),
        compiler_params=pltpu.CompilerParams(vmem_limit_bytes=VMEM_LIMIT),
        cost_estimate=pl.CostEstimate(flops=flops, bytes_accessed=moved, transcendentals=0),
    )(*args)


def shaped(shape, dtype):
    return jax.ShapeDtypeStruct(tuple(shape), dtype)


def swap_halves(part):
    lane = lax.broadcasted_iota(jnp.int32, part.shape, 1)
    return jnp.where(
        lane % HD < HD // 2,
        pltpu.roll(part, LANES - HD // 2, axis=1),
        pltpu.roll(part, HD // 2, axis=1),
    )


def rotated(values, cosine, signed_sine, sign):
    rows, width = values.shape
    parts = []
    for start in range(0, width, LANES):
        part = values[:, start : start + LANES]
        used = part.shape[1]
        if used < LANES:
            part = jnp.concatenate([part, jnp.zeros((rows, LANES - used), F32)], -1)
        turned = part * cosine + sign * (swap_halves(part) * signed_sine)
        parts.append(turned[:, :used])
    return jnp.concatenate(parts, -1)


def stacked_heads(ref, group):
    first = group * GROUPS
    return jnp.concatenate(
        [ref[:, (first + g) * HD : (first + g + 1) * HD] for g in range(GROUPS)], 0
    )


def kv_kernel(tokens, gain, weight, cosine, sine, normed_out, kv_out):
    values = tokens[...].astype(F32)
    scale = lax.rsqrt(jnp.mean(values * values, -1, keepdims=True) + EPS)
    normed = (values * scale * gain[...]).astype(BF16)
    normed_out[...] = normed
    linear = mm(normed, weight[...])
    kv_out[:, :KVW] = rotated(linear[:, :KVW], cosine[...], sine[...], 1.0).astype(BF16)
    kv_out[:, KVW:] = linear[:, KVW:].astype(BF16)


def query_kernel(normed, weight, cosine, sine, query_out):
    linear = mm(normed[...], weight[...])
    turned = rotated(linear, cosine[...], sine[...], 1.0) * (1.0 / math.sqrt(HD))
    query_out[...] = turned.astype(BF16)


def causal(scores, rows):
    key_pos = lax.broadcasted_iota(jnp.int32, scores.shape, 0)
    query_pos = lax.broadcasted_iota(jnp.int32, scores.shape, 1) % rows
    return jnp.where(query_pos >= key_pos, scores, NEGATIVE)


def forward_kernel(index, queries, kv_all, attended, lse_out, q_scr, acc_scr, max_scr, sum_scr):
    rows = queries.shape[0]
    here = index[0]
    for group in range(KV):
        q_scr[group] = stacked_heads(queries, group)
    acc_scr[...] = jnp.zeros_like(acc_scr)
    max_scr[...] = jnp.full_like(max_scr, NEGATIVE)
    sum_scr[...] = jnp.zeros_like(sum_scr)

    def block(j, masked):
        keys_at = pl.ds(pl.multiple_of(j * rows, rows), rows)
        for group in range(KV):
            keys = kv_all[keys_at, group * HD : (group + 1) * HD]
            values = kv_all[keys_at, KVW + group * HD : KVW + (group + 1) * HD]
            scores = mm(keys, q_scr[group], 1, 1)
            if masked:
                scores = causal(scores, rows)
            old_max = max_scr[group, 0:1, :]
            new_max = jnp.maximum(old_max, jnp.max(scores, 0, keepdims=True))
            weights = jnp.exp(scores - new_max)
            factor = jnp.exp(old_max - new_max)
            max_scr[group, 0:1, :] = new_max
            sum_scr[group, 0:1, :] = sum_scr[group, 0:1, :] * factor + jnp.sum(
                weights, 0, keepdims=True
            )
            acc_scr[group] = acc_scr[group] * factor + mm(values, weights.astype(BF16), 0, 0)

    def step(j, carry):
        block(j, False)
        return carry

    lax.fori_loop(0, here, step, 0)
    block(here, True)
    lse_out[...] = jnp.zeros_like(lse_out)
    for group in range(KV):
        total = sum_scr[group, 0:1, :]
        result = acc_scr[group] / total
        lse_out[group : group + 1, :] = max_scr[group, 0:1, :] + jnp.log(total)
        for g in range(GROUPS):
            head = group * GROUPS + g
            attended[:, head * HD : (head + 1) * HD] = result[:, g * rows : (g + 1) * rows].T


def rms_back(values, gain, grad):
    width = values.shape[-1]
    scale = lax.rsqrt(jnp.mean(values * values, -1, keepdims=True) + EPS)
    scaled = values * scale
    pulled = grad * gain
    along = jnp.sum(pulled * scaled, -1, keepdims=True) * (1.0 / width)
    return scale * (pulled - scaled * along), grad * scaled


def put_tiles(out, first_tile, first_row_width, grad):
    owners = out.shape[0]
    rows = grad.shape[0] // owners
    for tile in range(grad.shape[1] // LANES):
        part = grad[:, tile * LANES : (tile + 1) * LANES].astype(BF16)
        for owner in range(owners):
            start = first_row_width + (first_tile + tile) * rows
            out[owner, pl.ds(start, rows), :] = part[owner * rows : (owner + 1) * rows]


def ffn_kernel(
    tokens, attended, out_weight, gain, in_weight, down_weight, out_grad,
    layer_out, middle_grad_out, attended_grad_out, big_grads, out_weight_grad, gain_grad,
    result_scr, back_scr, hidden_grad_scr,
):
    ff = down_weight.shape[0]
    owners = big_grads.shape[0]
    in_rows = in_weight.shape[0] // owners
    down_rows = ff // owners
    steps = ff // FF_STEP
    attended_low = attended[...].astype(BF16)
    middle = tokens[...].astype(F32) + mm(attended_low, out_weight[...])
    scale = lax.rsqrt(jnp.mean(middle * middle, -1, keepdims=True) + EPS)
    normed = (middle * scale * gain[...]).astype(BF16)
    grad_rows = out_grad[...]
    result_scr[...] = middle
    back_scr[...] = jnp.zeros_like(back_scr)
    tiles_per_step = FF_STEP // LANES
    width = grad_rows.shape[1]
    down_base = 2 * (ff // LANES) * in_rows

    for step in range(steps):
        gate_at = slice(step * FF_STEP, (step + 1) * FF_STEP)
        up_at = slice(ff + step * FF_STEP, ff + (step + 1) * FF_STEP)
        gate = mm(normed, in_weight[:, gate_at])
        up = mm(normed, in_weight[:, up_at])
        gated = 1.0 / (1.0 + jnp.exp(-gate))
        silu = gate * gated
        hidden = (silu * up).astype(BF16)
        down = down_weight[gate_at, :]
        result_scr[...] += mm(hidden, down)
        hidden_grad = mm(grad_rows, down, 1, 1)
        gate_grad = (hidden_grad * up * (gated * (1.0 + gate * (1.0 - gated)))).astype(BF16)
        up_grad = (hidden_grad * silu).astype(BF16)
        back_scr[...] += mm(gate_grad, in_weight[:, gate_at], 1, 1) + mm(
            up_grad, in_weight[:, up_at], 1, 1
        )
        put_tiles(big_grads, step * tiles_per_step, 0, mm(normed, gate_grad, 0, 0))
        put_tiles(big_grads, ff // LANES + step * tiles_per_step, 0, mm(normed, up_grad, 0, 0))
        hidden_grad_scr[gate_at, :] = mm(hidden, grad_rows, 0, 0)

    whole = width // LANES
    put_tiles(big_grads, 0, down_base, hidden_grad_scr[:, : whole * LANES])
    half = down_rows // 2
    for owner in range(owners):
        rest = hidden_grad_scr[owner * down_rows : (owner + 1) * down_rows, whole * LANES :]
        rest = jnp.concatenate([rest[:half], rest[half:]], -1).astype(BF16)
        big_grads[owner, pl.ds(down_base + whole * down_rows, half), :] = rest

    layer_out[...] = result_scr[...].astype(BF16)
    middle_back, gain_terms = rms_back(middle, gain[...], back_scr[...])
    gain_grad[...] = jnp.sum(gain_terms, 0, keepdims=True)
    middle_grad = middle_back + grad_rows.astype(F32)
    middle_grad_out[...] = middle_grad
    branch = middle_grad.astype(BF16)
    out_weight_grad[...] = mm(attended_low, branch, 0, 0).astype(BF16)
    attended_grad_out[...] = mm(branch, out_weight[...], 1, 1).astype(BF16)


def backward_kernel(
    index, queries, kv_all, attended, attended_grad, lse, normed, query_weight, cosine, sine,
    kv_grads, query_weight_grad, normed_grad,
    q_scr, g_scr, delta_scr, acc_scr, query_grad_scr,
):
    rows = queries.shape[0]
    blocks = kv_all.shape[0] // rows
    here = index[0]
    for group in range(KV):
        q_scr[group] = stacked_heads(queries, group)
        grads = stacked_heads(attended_grad, group)
        g_scr[group] = grads
        terms = (grads.astype(F32) * stacked_heads(attended, group)).T
        delta_scr[group, 0:1, :] = jnp.sum(terms, 0, keepdims=True)
    acc_scr[...] = jnp.zeros_like(acc_scr)

    def block(j, masked):
        keys_at = pl.ds(pl.multiple_of(j * rows, rows), rows)
        for group in range(KV):
            key_lanes = slice(group * HD, (group + 1) * HD)
            value_lanes = slice(KVW + group * HD, KVW + (group + 1) * HD)
            keys = kv_all[keys_at, key_lanes]
            values = kv_all[keys_at, value_lanes]
            group_q = q_scr[group]
            group_g = g_scr[group]
            scores = mm(keys, group_q, 1, 1)
            if masked:
                scores = causal(scores, rows)
            prob = jnp.exp(scores - lse[group : group + 1, :])
            prob_grad = mm(values, group_g, 1, 1)
            score_grad = (prob * (prob_grad - delta_scr[group, 0:1, :])).astype(BF16)
            kv_grads[keys_at, value_lanes] = mm(prob.astype(BF16), group_g).astype(BF16)
            kv_grads[keys_at, key_lanes] = mm(score_grad, group_q).astype(BF16)
            acc_scr[group] += mm(keys, score_grad, 0, 0)

    def step(j, carry):
        block(j, False)
        return carry

    def clear(j, carry):
        keys_at = pl.ds(pl.multiple_of(j * rows, rows), rows)
        kv_grads[keys_at, :] = jnp.zeros((rows, kv_grads.shape[1]), BF16)
        return carry

    lax.fori_loop(0, here, step, 0)
    block(here, True)
    lax.fori_loop(here + 1, blocks, clear, 0)
    for group in range(KV):
        for g in range(GROUPS):
            head = group * GROUPS + g
            part = acc_scr[group, :, g * rows : (g + 1) * rows]
            query_grad_scr[:, head * HD : (head + 1) * HD] = part.T
    back = rotated(query_grad_scr[...], cosine[...], sine[...], -1.0) * (1.0 / math.sqrt(HD))
    back = back.astype(BF16)
    query_weight_grad[...] = mm(normed[...], back, 0, 0).astype(BF16)
    normed_grad[...] = mm(back, query_weight[...], 1, 1)


def tail_kernel(
    kv_parts, tokens, gain, normed, normed_grad, middle_grad, kv_weight, cosine, sine,
    tokens_grad, kv_weight_grad, gain_grad,
):
    rows = tokens.shape[0]
    parts = kv_parts.shape[0] // rows

    def add(j, total):
        return total + kv_parts[pl.ds(pl.multiple_of(j * rows, rows), rows), :].astype(F32)

    kv_grad = lax.fori_loop(0, parts, add, jnp.zeros((rows, 2 * KVW), F32))
    key_back = rotated(kv_grad[:, :KVW], cosine[...], sine[...], -1.0)
    back = jnp.concatenate([key_back, kv_grad[:, KVW:]], -1).astype(BF16)
    kv_weight_grad[...] = mm(normed[...], back, 0, 0).astype(BF16)
    total = normed_grad[...] + mm(back, kv_weight[...], 1, 1)
    values = tokens[...].astype(F32)
    input_grad, gain_terms = rms_back(values, gain[...], total)
    gain_grad[...] = jnp.sum(gain_terms, 0, keepdims=True)
    tokens_grad[...] = (middle_grad[...] + input_grad).astype(BF16)


def swap(value, axis, bit):
    count = lax.axis_size(axis)
    return lax.ppermute(value, axis, [(i, i ^ (1 << bit)) for i in range(count)])


def own_bit(axis, bit):
    return (lax.axis_index(axis) >> bit) & 1


def halved(value, axis, bit, dim):
    mine = own_bit(axis, bit)
    keep = lax.dynamic_index_in_dim(value, mine, dim, keepdims=False)
    send = lax.dynamic_index_in_dim(value, 1 - mine, dim, keepdims=False)
    got = swap(send, axis, bit)
    return (keep.astype(F32) + got.astype(F32)).astype(value.dtype)


def doubled(value, axis, bit, dim):
    mine = own_bit(axis, bit)
    got = swap(value, axis, bit)
    low = jnp.where(mine == 0, value, got)
    high = jnp.where(mine == 0, got, value)
    return jnp.stack([low, high], dim)


def scattered_ws(value):
    split = value.reshape((2, 2) + value.shape[1:])
    return halved(halved(split, "ws", 0, 1), "ws", 1, 0)


def summed_ctx(value, high_first):
    count = lax.axis_size("ctx")
    bits = count.bit_length() - 1
    rows = value.shape[0]
    split = value.reshape((2,) * bits + (rows // count, value.shape[1]))
    order = list(range(bits))
    if high_first:
        order.reverse()
    left = list(range(bits - 1, -1, -1))
    dims = []
    for bit in order:
        dim = left.index(bit)
        left.pop(dim)
        dims.append(dim)
        split = halved(split, "ctx", bit, dim)
    for bit, dim in zip(reversed(order), reversed(dims)):
        split = doubled(split, "ctx", bit, dim)
    return split.reshape(rows, value.shape[1])


def untiled(tiles, rows):
    count = tiles.shape[0] // rows
    return jnp.concatenate([tiles[i * rows : (i + 1) * rows] for i in range(count)], -1)


def by_owner(grad, owners):
    rows = grad.shape[0] // owners
    split = grad.reshape(owners, rows, grad.shape[1])
    return jnp.concatenate(
        [split[:, :, at : at + LANES] for at in range(0, grad.shape[1], LANES)], 1
    )


def body(
    tokens,
    attn_gain,
    query_weight,
    key_weight,
    value_weight,
    output_weight,
    ffn_gain,
    gate_weight,
    up_weight,
    down_weight,
    out_grad,
):
    seq_count, rows, width = tokens.shape
    ctx_count = lax.axis_size("ctx")
    owners = lax.axis_size("ws")
    ctx_index = lax.axis_index("ctx")
    slice_rows = query_weight.shape[0]
    ff = gate_weight.shape[1]
    tokens = tokens.reshape(rows, width)
    out_grad = out_grad.reshape(rows, width)
    index = jnp.full((1,), ctx_index, jnp.int32)

    gains = jnp.stack([attn_gain, ffn_gain], -1)
    packed = jnp.concatenate(
        [key_weight, value_weight, jnp.pad(gains, ((0, 0), (0, LANES - 2)))], -1
    )
    kv_full = lax.all_gather(packed, "ws", axis=0, tiled=True)
    full_query = lax.all_gather(query_weight, "ws", axis=0, tiled=True)
    full_output = lax.all_gather(output_weight, "ws", axis=0, tiled=True)
    full_in = lax.all_gather(
        jnp.concatenate([gate_weight, up_weight], -1), "ws", axis=0, tiled=True
    )
    full_down = lax.all_gather(down_weight, "ws", axis=0, tiled=True)
    full_kv = kv_full[:, : 2 * KVW]
    gain_rows = kv_full[:, 2 * KVW : 2 * KVW + 2].T.astype(F32)
    gain_attn = gain_rows[0:1]
    gain_ffn = gain_rows[1:2]

    positions = (ctx_index * rows + jnp.arange(rows, dtype=jnp.int32)).astype(F32)
    frequency = jnp.exp(jnp.arange(HD // 2).astype(F32) * (-2.0 * math.log(THETA) / HD))
    angles = positions[:, None] * frequency[None, :]
    cosine = jnp.cos(angles)
    sine = jnp.sin(angles)
    cosine = jnp.concatenate([cosine] * 4, -1)
    sine = jnp.concatenate([-sine, sine] * 2, -1)

    normed, kv_own = call(
        kv_kernel,
        (shaped((rows, width), BF16), shaped((rows, 2 * KVW), BF16)),
        (tokens, gain_attn, full_kv, cosine, sine),
        flops=2 * rows * width * 2 * KVW,
    )
    queries = call(
        query_kernel,
        shaped((rows, width), BF16),
        (normed, full_query, cosine, sine),
        flops=2 * rows * width * width,
    )
    kv_all = lax.all_gather(kv_own, "ctx", axis=0, tiled=True)

    attended, lse = call(
        forward_kernel,
        (shaped((rows, width), F32), shaped((8, GROUPS * rows), F32)),
        (index, queries, kv_all),
        scratch=(
            pltpu.VMEM((KV, GROUPS * rows, HD), BF16),
            pltpu.VMEM((KV, HD, GROUPS * rows), F32),
            pltpu.VMEM((KV, 8, GROUPS * rows), F32),
            pltpu.VMEM((KV, 8, GROUPS * rows), F32),
        ),
        flops=4 * rows * ctx_count * rows * width,
        smem=1,
    )

    tile_rows = (2 * slice_rows * ff + (ff // owners) * width) // LANES
    layer_out, middle_grad, attended_grad, big_grads, output_weight_grad, ffn_gain_grad = call(
        ffn_kernel,
        (
            shaped((rows, width), BF16),
            shaped((rows, width), F32),
            shaped((rows, width), BF16),
            shaped((owners, tile_rows, LANES), BF16),
            shaped((width, width), BF16),
            shaped((1, width), F32),
        ),
        (tokens, attended, full_output, gain_ffn, full_in, full_down, out_grad),
        scratch=(
            pltpu.VMEM((rows, width), F32),
            pltpu.VMEM((rows, width), F32),
            pltpu.VMEM((ff, width), F32),
        ),
        flops=18 * rows * width * ff,
    )

    big_slice = scattered_ws(big_grads)

    kv_grads, query_weight_grad, normed_grad = call(
        backward_kernel,
        (
            shaped((ctx_count * rows, 2 * KVW), BF16),
            shaped((width, width), BF16),
            shaped((rows, width), F32),
        ),
        (
            index, queries, kv_all, attended, attended_grad, lse, normed, full_query, cosine, sine,
        ),
        scratch=(
            pltpu.VMEM((KV, GROUPS * rows, HD), BF16),
            pltpu.VMEM((KV, GROUPS * rows, HD), BF16),
            pltpu.VMEM((KV, 8, GROUPS * rows), F32),
            pltpu.VMEM((KV, HD, GROUPS * rows), F32),
            pltpu.VMEM((rows, width), F32),
        ),
        flops=10 * rows * ctx_count * rows * width,
        smem=1,
    )

    kv_parts = lax.all_to_all(kv_grads, "ctx", split_axis=0, concat_axis=0, tiled=True)
    tokens_grad, kv_weight_grad, attn_gain_grad = call(
        tail_kernel,
        (
            shaped((rows, width), BF16),
            shaped((width, 2 * KVW), BF16),
            shaped((1, width), F32),
        ),
        (
            kv_parts, tokens, gain_attn, normed, normed_grad, middle_grad, full_kv, cosine, sine,
        ),
        flops=4 * rows * width * 2 * KVW,
    )

    big_total = summed_ctx(big_slice, True)
    gain_tile = jnp.concatenate([attn_gain_grad, ffn_gain_grad], 0).astype(BF16)
    gain_tile = gain_tile.reshape(2, owners, slice_rows).transpose(1, 0, 2).reshape(owners, -1)
    gain_tile = jnp.pad(gain_tile, ((0, 0), (0, 64 * LANES - 2 * slice_rows)))
    small_grads = jnp.concatenate(
        [
            by_owner(
                jnp.concatenate([query_weight_grad, output_weight_grad, kv_weight_grad], -1),
                owners,
            ),
            gain_tile.reshape(owners, 64, LANES),
        ],
        1,
    )
    small_total = summed_ctx(scattered_ws(small_grads), False)

    in_rows = ff // LANES * slice_rows
    down_rows = ff // owners
    whole = width // LANES
    gate_weight_grad = untiled(big_total[:in_rows], slice_rows)
    up_weight_grad = untiled(big_total[in_rows : 2 * in_rows], slice_rows)
    down_tiles = big_total[2 * in_rows :]
    rest = down_tiles[whole * down_rows :]
    half = LANES // 2
    down_weight_grad = jnp.concatenate(
        [
            untiled(down_tiles[: whole * down_rows], down_rows),
            jnp.concatenate([rest[:, :half], rest[:, half:]], 0),
        ],
        -1,
    )
    small = untiled(small_total[:-64], slice_rows)
    gain_out = small_total[-64:].reshape(-1)
    outs = (
        gain_out[:slice_rows],
        small[:, :width],
        small[:, 2 * width : 2 * width + KVW],
        small[:, 2 * width + KVW :],
        small[:, width : 2 * width],
        gain_out[slice_rows : 2 * slice_rows],
        gate_weight_grad,
        up_weight_grad,
        down_weight_grad,
    )
    return (
        layer_out.reshape(seq_count, rows, width),
        tokens_grad.reshape(seq_count, rows, width),
    ) + tuple(value.astype(F32) for value in outs)


def solution(mesh):
    in_specs = (
        P("ws", "ctx", None),
        P("ws"),
        P("ws", None),
        P("ws", None),
        P("ws", None),
        P("ws", None),
        P("ws"),
        P("ws", None),
        P("ws", None),
        P("ws", None),
        P("ws", "ctx", None),
    )
    out_specs = (
        P("ws", "ctx", None),
        P("ws", "ctx", None),
        P("ws"),
        P("ws", None),
        P("ws", None),
        P("ws", None),
        P("ws", None),
        P("ws"),
        P("ws", None),
        P("ws", None),
        P("ws", None),
    )
    return jax.shard_map(body, mesh=mesh, in_specs=in_specs, out_specs=out_specs, check_vma=False)
```

time: 652 us -> 358 us (0.55)
  blocking collectives: 193 us -> 26.9 us
  waiting for transfers between devices: 301 us -> 215 us
  matrix products: 40.3 us -> 0 us
  starting transfers between devices: 66.7 us -> 27 us
  Pallas kernels: 0 us -> 35.8 us
  other arithmetic: 7.94 us -> 17.5 us
    psum x1 -> x0, blocking collectives: 150 us -> none  [body(): lax.psum((share_attn, share_query, share_key, share_value, share_output,...]
    reduce_scatter x6 -> x0, waiting for transfers between devices: 129 us -> none  [the longest x1 32 us: body(): lax.psum_scatter(up_weight_grad.astype(jnp.bfloat16), 'ws', scatter_dimen...]
    ppermute x16, starting transfers between devices: 66 us -> 10.2 us  [swap(): return lax.ppermute(value, axis, [(i, i ^ 1 << bit) for i in range(count)])]
    ppermute x16, waiting for transfers between devices: 59.8 us -> 110 us  [swap(): return lax.ppermute(value, axis, [(i, i ^ 1 << bit) for i in range(count)])]
    dot_general x28 -> x0, matrix products: 40.3 us -> none  [the longest x1 4.75 us: body(): jnp.einsum('nd,fd->nf', grad_rows, full_down, preferred_element_type=jnp....]
    pallas_call x0 -> x6, Pallas kernels: none -> 35.8 us  [call(): pl.pallas_call(kernel, out_shape=outs, in_specs=[SMEM_SPEC] * smem + [VME...]
    unnamed x12 -> x3, waiting for transfers between devices: 35.3 us -> 0.05 us
    all_to_all x0 -> x1, waiting for transfers between devices: none -> 33.9 us  [body(): lax.all_to_all(kv_grads, 'ctx', split_axis=0, concat_axis=0, tiled=True)]
  transfers between devices with their start and end apart: 27 -> 20, of which waited for: 21 -> 16; matrix products, arithmetic and copies ran while one was open for 5% -> 7% of each run, Pallas kernels for 0% -> 3%
where the time goes in v1:
time: 358 us
  waiting for transfers between devices  215 us (60%)
  Pallas kernels  35.8 us (10%)
  starting transfers between devices  27 us (8%)
  blocking collectives  26.9 us (8%)
  local copies, waits for them, and re-layouts  20.6 us (6%)
  other arithmetic  17.5 us (5%)
  between operations  14.5 us (4%)
    ppermute x16, waiting for transfers between devices, swap(): return lax.ppermute(value, axis, [(i, i ^ 1 << bit) for i in range(count)])  110 us
    pallas_call x6, Pallas kernels, call(): pl.pallas_call(kernel, out_shape=outs, in_specs=[SMEM_SPEC] * smem + [VME...  35.8 us
    all_to_all x1, waiting for transfers between devices, body(): lax.all_to_all(kv_grads, 'ctx', split_axis=0, concat_axis=0, tiled=True)  33.9 us
    all_gather x1, waiting for transfers between devices, body(): lax.all_gather(jnp.concatenate([gate_weight, up_weight], -1), 'ws', axis=...  32.9 us
    all_gather x1, waiting for transfers between devices, body(): kv_all = lax.all_gather(kv_own, 'ctx', axis=0, tiled=True)  20.5 us
    all_gather x1, waiting for transfers between devices, body(): full_down = lax.all_gather(down_weight, 'ws', axis=0, tiled=True)  18.3 us
    all_to_all x1, starting transfers between devices, body(): lax.all_to_all(kv_grads, 'ctx', split_axis=0, concat_axis=0, tiled=True)  16.7 us
    ppermute x16, starting transfers between devices, swap(): return lax.ppermute(value, axis, [(i, i ^ 1 << bit) for i in range(count)])  10.2 us
  transfers between devices with their start and end apart: 20, of which 16 were waited for; matrix products, arithmetic and copies ran while one was open for 7% of the time, Pallas kernels for 3%

profile of v1, /device:TPU:0, one launch (start us, length us, event | category | flops | bytes accessed | tf_op | source)
XLA Modules:
  0.0 357.5 jit_solution(12429319499573265797)
XLA Ops:
  7.2 0.7 stack.63
  7.9 0.7 stack.64
  8.7 1.0 fusion.10
  9.8 9.1 %all_gather.18 = bf16[576,512]{1,0:T(8,128)(2,1)S(1)} all-gather(bf16[144,512]{1,0:T(8,128)(2,1)S(1)} %fusion.10), channel_id=1, replica_groups=mesh['ctx'=8,'ws'=4] {'ws'}, dimensions={0}, use_global_device_ids=true | all-gather | bytes 737280 | tf_op jit(solution)/shard_map/all_gather | solution.py:394
  18.9 0.8 slice.316.weight.kv_weight
  19.9 0.7 copy.83.gain
  20.6 0.9 copy.80
  22.0 1.0 pad_maximum_fusion.6
  23.0 2.5 shard_map.194
  25.5 1.0 copy.84
  26.7 1.0 pad_maximum_fusion.1
  27.7 0.7 copy.86.gain
  28.4 0.9 copy.85
  29.4 8.9 %all_gather.19.weight.query_weight = bf16[576,576]{1,0:T(8,128)(2,1)} all-gather(bf16[144,576]{1,0:T(8,128)(2,1)S(1)} %copy-done.12), channel_id=1, replica_groups=mesh['ctx'=8,'ws'=4] {'ws'}, dimensions={0}, use_global_device_ids=true | all-gather | bytes 829440 | tf_op jit(solution)/shard_map/all_gather | solution.py:395
  38.2 2.7 shard_map.195.queries
  41.0 8.9 %all_gather.21.out_weight = bf16[576,576]{1,0:T(8,128)(2,1)} all-gather(bf16[144,576]{1,0:T(8,128)(2,1)S(1)} %copy-done.13), channel_id=1, replica_groups=mesh['ctx'=8,'ws'=4] {'ws'}, dimensions={0}, use_global_device_ids=true | all-gather | bytes 829440 | tf_op jit(solution)/shard_map/all_gather | solution.py:396
  49.9 20.5 %all-gather.4.cloned.1.call-done.kv_all = bf16[2048,384]{1,0:T(8,128)(2,1)} async-done(((bf16[256,384]{1,0:T(8,128)(2,1)}), bf16[2048,384]{1,0:T(8,128)(2,1)}) %all-gather.4.cloned.1.call-update) | async-done | bytes 1572880 | tf_op jit(solution)/shard_map/all_gather | solution.py:426
  70.4 4.6 %shard_map.196 = (f32[256,576]{1,0:T(8,128)}, f32[8,768]{1,0:T(8,128)}) custom-call(s32[1]{0:T(128)} %bitcast.1.index, bf16[256,576]{1,0:T(8,128)(2,1)} %shard_map.195.queries, bf16[2048,384]{1,0:T(8,128)(2,1)} %all-gather.4.cloned.1.call-done.kv_all), custom_call_target="tpu_custom_call" | custom-call | flops 1207959552 | tf_op jit(solution)/shard_map/pallas_call | solution.py:38
  74.9 18.3 %all-gather.8.cloned.1.call-done.down_weight = bf16[1536,576]{1,0:T(8,128)(2,1)} async-done(((bf16[384,576]{1,0:T(8,128)(2,1)}), bf16[1536,576]{1,0:T(8,128)(2,1)}) %all-gather.8.cloned.1.call-update) | async-done | bytes 1769488 | tf_op jit(solution)/shard_map/all_gather | solution.py:400
  93.2 32.9 %all-gather.6.cloned.1.call-done.in_weight = bf16[576,3072]{1,0:T(8,128)(2,1)} async-done(((bf16[144,3072]{1,0:T(8,128)(2,1)}), bf16[576,3072]{1,0:T(8,128)(2,1)}) %all-gather.6.cloned.1.call-update) | async-done | bytes 3538960 | tf_op jit(solution)/shard_map/all_gather | solution.py:397
  126.1 14.0 %shard_map.197 = (bf16[256,576]{1,0:T(8,128)(2,1)}, f32[256,576]{1,0:T(8,128)}, bf16[256,576]{1,0:T(8,128)(2,1)}, bf16[4,5184,128]{2,1,0:T(8,128)(2,1)}, bf16[576,576]{1,0:T(8,128)(2,1)}, /*index=5*/f32[1,576]{1,0:T(1,128)}) custom-call(bf16[256,576]{1,0:T(8,128)(2,1)} %bitcast.133, f32[256,576]{1,0:T(8,128)} %get-tuple-element.29.attended, ...), custom_call_target="tpu_custom_call" | custom-call | flops 4076863488 | tf_op jit(solution)/shard_map/pallas_call | solution.py:38
  140.2 7.6 %shard_map.198 = (bf16[2048,384]{1,0:T(8,128)(2,1)}, bf16[576,576]{1,0:T(8,128)(2,1)}, f32[256,576]{1,0:T(8,128)}) custom-call(s32[1]{0:T(128)} %bitcast.1.index, bf16[256,576]{1,0:T(8,128)(2,1)} %shard_map.195.queries, bf16[2048,384]{1,0:T(8,128)(2,1)} %all-gather.4.cloned.1.call-done.kv_all, f32[256,576]{1,0:T(8,128)} %get-tuple-element.29.attended, ...), custom_call_target="tpu_custom_call" | custom-call | flops 3019898880 | tf_op jit(solution)/shard_map/pallas_call | solution.py:38
  147.8 16.7 %all-to-all-start = ((bf16[8,256,384]{2,1,0:T(8,128)(2,1)}), bf16[8,256,384]{2,1,0:T(8,128)(2,1)S(1)}, u32[]{:S(2)}, u32[]{:S(2)}) async-start(bf16[8,256,384]{2,1,0:T(8,128)(2,1)} %bitcast.143), calls=%async_computation | async-start | bytes 3145728 | tf_op jit(solution)/shard_map/all_to_all | solution.py:485
  164.5 3.4 dynamic-slice_bitcast_fusion
  168.0 33.9 %all-to-all-done = bf16[8,256,384]{2,1,0:T(8,128)(2,1)S(1)} async-done(((bf16[8,256,384]{2,1,0:T(8,128)(2,1)}), bf16[8,256,384]{2,1,0:T(8,128)(2,1)S(1)}, u32[]{:S(2)}, u32[]{:S(2)}) %all-to-all-start) | async-done | bytes 1572896 | tf_op jit(solution)/shard_map/all_to_all | solution.py:485
  201.9 1.2 copy-done
  203.2 4.5 %shard_map.199 = (bf16[256,576]{1,0:T(8,128)(2,1)}, bf16[576,384]{1,0:T(8,128)(2,1)}, f32[1,576]{1,0:T(1,128)}) custom-call(bf16[2048,384]{1,0:T(8,128)(2,1)} %bitcast.110, bf16[256,576]{1,0:T(8,128)(2,1)} %bitcast.134, f32[1,576]{1,0:T(1,128)} %copy.83.gain, bf16[256,576]{1,0:T(8,128)(2,1)} %get-tuple-element.27.normed, ...), custom_call_target="tpu_custom_call" | custom-call | flops 226492416 | tf_op jit(solution)/shard_map/pallas_call | solution.py:38
  207.6 0.7 convert_reduce_fusion.1
  208.6 2.4 concatenate.83
  212.0 3.2 fusion
  215.5 0.6 collective-permute-start.1
  216.2 1.2 dynamic-slice_bitcast_fusion.1
  217.3 1.5 collective-permute-start.9
  218.8 10.1 %collective-permute-done.1 = bf16[1792,128]{1,0:T(8,128)(2,1)S(1)} collective-permute-done((bf16[1792,128]{1,0:T(8,128)(2,1)S(1)}, bf16[1792,128]{1,0:T(8,128)(2,1)S(1)}, u32[]{:S(2)}, u32[]{:S(2)}) %collective-permute-start.1) | collective-permute-done | bytes 458784 | tf_op jit(solution)/shard_map/ppermute | solution.py:306
  229.1 1.5 collective-permute-start.2
  230.6 5.4 %collective-permute-done.2 = bf16[2,2,224,128]{3,2,1,0:T(8,128)(2,1)} collective-permute-done((bf16[2,2,224,128]{3,2,1,0:T(8,128)(2,1)S(1)}, bf16[2,2,224,128]{3,2,1,0:T(8,128)(2,1)}, u32[]{:S(2)}, u32[]{:S(2)}) %collective-permute-start.2) | collective-permute-done | bytes 229408 | tf_op jit(solution)/shard_map/ppermute | solution.py:306
  236.0 1.0 fusion.6
  237.2 4.8 %collective-permute-done.3 = bf16[2,224,128]{2,1,0:T(8,128)(2,1)S(1)} collective-permute-done((bf16[2,224,128]{2,1,0:T(8,128)(2,1)S(1)}, bf16[2,224,128]{2,1,0:T(8,128)(2,1)S(1)}, u32[]{:S(2)}, u32[]{:S(2)}) %collective-permute-start.3) | collective-permute-done | bytes 114720 | tf_op jit(solution)/shard_map/ppermute | solution.py:306
  242.0 0.9 collective-permute-start.4
  242.9 14.2 %collective-permute-done.9 = bf16[5184,128]{1,0:T(8,128)(2,1)} collective-permute-done((bf16[5184,128]{1,0:T(8,128)(2,1)}, bf16[5184,128]{1,0:T(8,128)(2,1)}, u32[]{:S(2)}, u32[]{:S(2)}) %collective-permute-start.9) | collective-permute-done | bytes 1327136 | tf_op jit(solution)/shard_map/ppermute | solution.py:306
  257.1 1.7 fusion.1
  258.9 0.9 copy-done.1
  259.8 2.1 collective-permute-start.10
  261.9 15.7 %collective-permute-done.5 = bf16[224,128]{1,0:T(8,128)(2,1)S(1)} collective-permute-done((bf16[224,128]{1,0:T(8,128)(2,1)S(1)}, bf16[224,128]{1,0:T(8,128)(2,1)S(1)}, u32[]{:S(2)}, u32[]{:S(2)}) %collective-permute-start.5) | collective-permute-done | bytes 57376 | tf_op jit(solution)/shard_map/ppermute | solution.py:306
  277.7 0.9 copy.91
  278.6 0.9 copy.92
  279.5 14.4 %collective-permute-done.6 = bf16[2,224,128]{2,1,0:T(8,128)(2,1)} collective-permute-done((bf16[2,224,128]{2,1,0:T(8,128)(2,1)S(1)}, bf16[2,224,128]{2,1,0:T(8,128)(2,1)}, u32[]{:S(2)}, u32[]{:S(2)}) %collective-permute-start.6) | collective-permute-done | bytes 114720 | tf_op jit(solution)/shard_map/ppermute | solution.py:306
  293.9 0.9 select_bitcast_fusion.9
  294.9 1.1 collective-permute-start.7
  296.3 4.7 %collective-permute-done.7 = bf16[2,2,224,128]{3,2,0,1:T(8,128)(2,1)S(1)} collective-permute-done((bf16[2,2,224,128]{3,2,0,1:T(8,128)(2,1)S(1)}, bf16[2,2,224,128]{3,2,0,1:T(8,128)(2,1)S(1)}, u32[]{:S(2)}, u32[]{:S(2)}) %collective-permute-start.7) | collective-permute-done | bytes 229408 | tf_op jit(solution)/shard_map/ppermute | solution.py:306
  301.2 2.2 collective-permute-done.11
  303.5 1.1 collective-permute-start.12
  304.6 5.2 %collective-permute-done.12 = bf16[648,128]{1,0:T(8,128)(2,1)S(1)} collective-permute-done((bf16[648,128]{1,0:T(8,128)(2,1)S(1)}, bf16[648,128]{1,0:T(8,128)(2,1)S(1)}, u32[]{:S(2)}, u32[]{:S(2)}) %collective-permute-start.12) | collective-permute-done | bytes 165920 | tf_op jit(solution)/shard_map/ppermute | solution.py:306
  310.3 4.9 %collective-permute-done.13 = bf16[648,128]{1,0:T(8,128)(2,1)S(1)} collective-permute-done((bf16[648,128]{1,0:T(8,128)(2,1)S(1)}, bf16[648,128]{1,0:T(8,128)(2,1)S(1)}, u32[]{:S(2)}, u32[]{:S(2)}) %collective-permute-start.13) | collective-permute-done | bytes 165920 | tf_op jit(solution)/shard_map/ppermute | solution.py:306
  315.4 0.8 fusion.12
  316.2 9.8 %collective-permute-done.14 = bf16[2,648,128]{2,1,0:T(8,128)(2,1)S(1)} collective-permute-done((bf16[2,648,128]{2,1,0:T(8,128)(2,1)S(1)}, bf16[2,648,128]{2,1,0:T(8,128)(2,1)S(1)}, u32[]{:S(2)}, u32[]{:S(2)}) %collective-permute-start.14) | collective-permute-done | bytes 331808 | tf_op jit(solution)/shard_map/ppermute | solution.py:306
  326.1 0.6 collective-permute-start.15
  326.7 0.6 slice_convert_fusion.2
  327.3 0.9 slice_convert_fusion
  328.2 0.8 slice_convert_fusion.1
  328.9 18.1 %collective-permute-done.15 = bf16[2,2,648,128]{3,2,1,0:T(8,128)(2,1)S(1)} collective-permute-done((bf16[2,2,648,128]{3,2,1,0:T(8,128)(2,1)S(1)}, bf16[2,2,648,128]{3,2,1,0:T(8,128)(2,1)S(1)}, u32[]{:S(2)}, u32[]{:S(2)}) %collective-permute-start.15) | collective-permute-done | bytes 663584 | tf_op jit(solution)/shard_map/ppermute | solution.py:306
  347.6 1.1 copy.93
  349.0 1.0 convert_element_type.223
  350.0 1.0 convert_element_type.224
  (125 shorter events, 5.2 us)
Async XLA Ops:
  7.2 63.2 %all-gather.4.cloned.1.call-start = ((), (), s32[]{:S(2)}) async-start(), calls=%async_computation.1 | async-start | bytes 1769472 | tf_op jit(solution)/shard_map/all_gather | solution.py:426
  9.7 10.8 %copy-start.10 = (bf16[1,256,576]{1,2,0:T(8,128)(2,1)S(1)}, bf16[1,256,576]{1,2,0:T(8,128)(2,1)}, u32[]{:S(2)}) copy-start(bf16[1,256,576]{1,2,0:T(8,128)(2,1)} %param.11) | copy-start | bytes 884740
  19.8 5.7 %copy-start.7 = (bf16[384,576]{0,1:T(8,128)(2,1)S(1)}, bf16[384,576]{0,1:T(8,128)(2,1)}, u32[]{:S(2)}) copy-start(bf16[384,576]{0,1:T(8,128)(2,1)} %param.20) | copy-start | bytes 1327108
  21.5 5.2 %copy-start.5 = (bf16[144,1536]{1,0:T(8,128)(2,1)S(1)}, bf16[144,1536]{1,0:T(8,128)(2,1)}, u32[]{:S(2)}) copy-start(bf16[144,1536]{1,0:T(8,128)(2,1)} %param.19) | copy-start | bytes 1327108
  21.5 5.2 %copy-start.6 = (bf16[144,1536]{1,0:T(8,128)(2,1)S(1)}, bf16[144,1536]{1,0:T(8,128)(2,1)}, u32[]{:S(2)}) copy-start(bf16[144,1536]{1,0:T(8,128)(2,1)} %param.18) | copy-start | bytes 1327108
  25.5 67.7 %all-gather.8.cloned.1.call-start = ((), (), s32[]{:S(2)}) async-start(), calls=%async_computation.3 | async-start | bytes 2457600 | tf_op jit(solution)/shard_map/all_gather | solution.py:400
  26.5 1.9 copy-start.11
  26.6 2.8 copy-start.12
  26.6 99.6 %all-gather.6.cloned.1.call-start = ((), (), s32[]{:S(2)}) async-start(), calls=%async_computation.2 | async-start | bytes 4423680 | tf_op jit(solution)/shard_map/all_gather | solution.py:397
  27.7 13.3 %copy-start.13 = (bf16[144,576]{1,0:T(8,128)(2,1)S(1)}, bf16[144,576]{1,0:T(8,128)(2,1)}, u32[]{:S(2)}) copy-start(bf16[144,576]{1,0:T(8,128)(2,1)} %param.16) | copy-start | bytes 497668
  147.8 54.2 %all-to-all-start = ((bf16[8,256,384]{2,1,0:T(8,128)(2,1)}), bf16[8,256,384]{2,1,0:T(8,128)(2,1)S(1)}, u32[]{:S(2)}, u32[]{:S(2)}) async-start(bf16[8,256,384]{2,1,0:T(8,128)(2,1)} %bitcast.143), calls=%async_computation | async-start | bytes 3145728 | tf_op jit(solution)/shard_map/all_to_all | solution.py:485
  164.5 3.4 copy-start.14
  167.9 44.0 %collective-permute-start.8 = (bf16[2,5184,128]{2,1,0:T(8,128)(2,1)}, bf16[2,5184,128]{2,1,0:T(8,128)(2,1)}, u32[]{:S(2)}, u32[]{:S(2)}) collective-permute-start(bf16[2,5184,128]{2,1,0:T(8,128)(2,1)} %dynamic-slice_bitcast_fusion), channel_id=1, source_target_pairs={{0,1},{1,0},{2,3},{3,2},{4,5},{5,4},{6,7},{7,6},{8,9},{9,8},{10,11... | collective-permute-start | bytes 7962632 | tf_op jit(solution)/shard_map/ppermute | solution.py:306
  201.9 1.2 copy-start
  203.2 5.4 %copy-start.3 = (bf16[576,576]{1,0:T(8,128)(2,1)S(1)}, bf16[576,576]{1,0:T(8,128)(2,1)}, u32[]{:S(2)}) copy-start(bf16[576,576]{1,0:T(8,128)(2,1)} %get-tuple-element.38) | copy-start | bytes 1990660
  203.2 5.4 %copy-start.4 = (bf16[576,576]{1,0:T(8,128)(2,1)S(1)}, bf16[576,576]{1,0:T(8,128)(2,1)}, u32[]{:S(2)}) copy-start(bf16[576,576]{1,0:T(8,128)(2,1)} %get-tuple-element.37) | copy-start | bytes 1990660
  211.9 3.3 collective-permute-start
  215.5 13.4 %collective-permute-start.1 = (bf16[1792,128]{1,0:T(8,128)(2,1)S(1)}, bf16[1792,128]{1,0:T(8,128)(2,1)S(1)}, u32[]{:S(2)}, u32[]{:S(2)}) collective-permute-start(bf16[1792,128]{1,0:T(8,128)(2,1)S(1)} %dynamic-slice_bitcast_fusion.4), channel_id=1, source_target_pairs={{0,2},{1,3},{2,0},{3,1},{4,6},{5,7},{6,4},{7,5},{8,10},{9,11},{10,... | collective-permute-start | bytes 1376264 | tf_op jit(solution)/shard_map/ppermute | solution.py:306
  217.3 39.7 %collective-permute-start.9 = (bf16[5184,128]{1,0:T(8,128)(2,1)}, bf16[5184,128]{1,0:T(8,128)(2,1)}, u32[]{:S(2)}, u32[]{:S(2)}) collective-permute-start(bf16[5184,128]{1,0:T(8,128)(2,1)} %dynamic-slice_bitcast_fusion.1), channel_id=1, source_target_pairs={{0,2},{1,3},{2,0},{3,1},{4,6},{5,7},{6,4},{7,5},{8,10},{9,11},{10,... | collective-permute-start | bytes 3981320 | tf_op jit(solution)/shard_map/ppermute | solution.py:306
  229.1 7.0 %collective-permute-start.2 = (bf16[2,2,224,128]{3,2,1,0:T(8,128)(2,1)S(1)}, bf16[2,2,224,128]{3,2,1,0:T(8,128)(2,1)}, u32[]{:S(2)}, u32[]{:S(2)}) collective-permute-start(bf16[2,2,224,128]{3,2,1,0:T(8,128)(2,1)S(1)} %dynamic-slice_bitcast_fusion.6), channel_id=1, source_target_pairs={{0,4},{4,0},{8,12},{12,8},{16,20},{20,16},{24,28},{28,24},{1,5},{5... | collective-permute-start | bytes 688136 | tf_op jit(solution)/shard_map/ppermute | solution.py:306
  237.1 4.9 %collective-permute-start.3 = (bf16[2,224,128]{2,1,0:T(8,128)(2,1)S(1)}, bf16[2,224,128]{2,1,0:T(8,128)(2,1)S(1)}, u32[]{:S(2)}, u32[]{:S(2)}) collective-permute-start(bf16[2,224,128]{2,1,0:T(8,128)(2,1)S(1)} %dynamic-slice_bitcast_fusion.8), channel_id=1, source_target_pairs={{0,8},{4,12},{8,0},{12,4},{16,24},{20,28},{24,16},{28,20},{1,9},{5... | collective-permute-start | bytes 344072 | tf_op jit(solution)/shard_map/ppermute | solution.py:306
  242.0 16.8 %collective-permute-start.4 = (bf16[224,128]{1,0:T(8,128)(2,1)S(1)}, bf16[224,128]{1,0:T(8,128)(2,1)S(1)}, u32[]{:S(2)}, u32[]{:S(2)}) collective-permute-start(bf16[224,128]{1,0:T(8,128)(2,1)S(1)} %dynamic-slice_bitcast_fusion.9), channel_id=1, source_target_pairs={{0,16},{4,20},{8,24},{12,28},{16,0},{20,4},{24,8},{28,12},{1,17},{... | collective-permute-start | bytes 172040 | tf_op jit(solution)/shard_map/ppermute | solution.py:306
  258.7 1.1 copy-start.1
  258.7 19.0 %copy-start.8 = (bf16[256,576]{1,0:T(8,128)(2,1)S(1)}, bf16[256,576]{1,0:T(8,128)(2,1)}, u32[]{:S(2)}) copy-start(bf16[256,576]{1,0:T(8,128)(2,1)} %get-tuple-element.30) | copy-start | bytes 884740
  258.7 19.9 %copy-start.9 = (bf16[256,576]{1,0:T(8,128)(2,1)S(1)}, bf16[256,576]{1,0:T(8,128)(2,1)}, u32[]{:S(2)}) copy-start(bf16[256,576]{1,0:T(8,128)(2,1)} %get-tuple-element.36) | copy-start | bytes 884740
  258.8 18.8 %collective-permute-start.5 = (bf16[224,128]{1,0:T(8,128)(2,1)S(1)}, bf16[224,128]{1,0:T(8,128)(2,1)S(1)}, u32[]{:S(2)}, u32[]{:S(2)}) collective-permute-start(bf16[224,128]{1,0:T(8,128)(2,1)S(1)} %fusion.11), channel_id=1, source_target_pairs={{0,16},{4,20},{8,24},{12,28},{16,0},{20,4},{24,8},{28,12},{1,17},{... | collective-permute-start | bytes 172040 | tf_op jit(solution)/shard_map/ppermute | solution.py:306
  259.8 36.1 %copy-start.2 = (bf16[5184,128]{1,0:T(8,128)(2,1)S(1)}, bf16[5184,128]{1,0:T(8,128)(2,1)}, u32[]{:S(2)}) copy-start(bf16[5184,128]{1,0:T(8,128)(2,1)} %copy-done.1) | copy-start | bytes 3981316
  259.8 36.1 %collective-permute-start.10 = (bf16[2,2,648,128]{3,2,1,0:T(8,128)(2,1)S(1)}, bf16[2,2,648,128]{3,2,1,0:T(8,128)(2,1)S(1)}, u32[]{:S(2)}, u32[]{:S(2)}) collective-permute-start(bf16[2,2,648,128]{3,2,1,0:T(8,128)(2,1)S(1)} %dynamic-slice_bitcast_fusion.3), channel_id=1, source_target_pairs={{0,16},{4,20},{8,24},{12,28},{16,0},{20,4},{24,8},{28,12},{1,17},{... | collective-permute-start | bytes 1990664 | tf_op jit(solution)/shard_map/ppermute | solution.py:306
  277.6 16.3 %collective-permute-start.6 = (bf16[2,224,128]{2,1,0:T(8,128)(2,1)S(1)}, bf16[2,224,128]{2,1,0:T(8,128)(2,1)}, u32[]{:S(2)}, u32[]{:S(2)}) collective-permute-start(bf16[2,224,128]{2,1,0:T(8,128)(2,1)S(1)} %pad_maximum_fusion.8), channel_id=1, source_target_pairs={{0,8},{4,12},{8,0},{12,4},{16,24},{20,28},{24,16},{28,20},{1,9},{5... | collective-permute-start | bytes 344072 | tf_op jit(solution)/shard_map/ppermute | solution.py:306
  294.9 6.1 %collective-permute-start.7 = (bf16[2,2,224,128]{3,2,0,1:T(8,128)(2,1)S(1)}, bf16[2,2,224,128]{3,2,0,1:T(8,128)(2,1)S(1)}, u32[]{:S(2)}, u32[]{:S(2)}) collective-permute-start(bf16[2,2,224,128]{3,2,0,1:T(8,128)(2,1)S(1)} %pad_maximum_fusion.5), channel_id=1, source_target_pairs={{0,4},{4,0},{8,12},{12,8},{16,20},{20,16},{24,28},{28,24},{1,5},{5... | collective-permute-start | bytes 688136 | tf_op jit(solution)/shard_map/ppermute | solution.py:306
  296.2 7.2 %collective-permute-start.11 = (bf16[2,648,128]{2,1,0:T(8,128)(2,1)S(1)}, bf16[2,648,128]{2,1,0:T(8,128)(2,1)S(1)}, u32[]{:S(2)}, u32[]{:S(2)}) collective-permute-start(bf16[2,648,128]{2,1,0:T(8,128)(2,1)S(1)} %dynamic-slice_bitcast_fusion.5), channel_id=1, source_target_pairs={{0,8},{4,12},{8,0},{12,4},{16,24},{20,28},{24,16},{28,20},{1,9},{5... | collective-permute-start | bytes 995336 | tf_op jit(solution)/shard_map/ppermute | solution.py:306
  303.5 6.3 %collective-permute-start.12 = (bf16[648,128]{1,0:T(8,128)(2,1)S(1)}, bf16[648,128]{1,0:T(8,128)(2,1)S(1)}, u32[]{:S(2)}, u32[]{:S(2)}) collective-permute-start(bf16[648,128]{1,0:T(8,128)(2,1)S(1)} %dynamic-slice_bitcast_fusion.7), channel_id=1, source_target_pairs={{0,4},{4,0},{8,12},{12,8},{16,20},{20,16},{24,28},{28,24},{1,5},{5... | collective-permute-start | bytes 497672 | tf_op jit(solution)/shard_map/ppermute | solution.py:306
  309.8 5.4 %collective-permute-start.13 = (bf16[648,128]{1,0:T(8,128)(2,1)S(1)}, bf16[648,128]{1,0:T(8,128)(2,1)S(1)}, u32[]{:S(2)}, u32[]{:S(2)}) collective-permute-start(bf16[648,128]{1,0:T(8,128)(2,1)S(1)} %fusion.7), channel_id=1, source_target_pairs={{0,4},{4,0},{8,12},{12,8},{16,20},{20,16},{24,28},{28,24},{1,5},{5... | collective-permute-start | bytes 497672 | tf_op jit(solution)/shard_map/ppermute | solution.py:306
  315.3 10.7 %collective-permute-start.14 = (bf16[2,648,128]{2,1,0:T(8,128)(2,1)S(1)}, bf16[2,648,128]{2,1,0:T(8,128)(2,1)S(1)}, u32[]{:S(2)}, u32[]{:S(2)}) collective-permute-start(bf16[2,648,128]{2,1,0:T(8,128)(2,1)S(1)} %pad_maximum_fusion.4), channel_id=1, source_target_pairs={{0,8},{4,12},{8,0},{12,4},{16,24},{20,28},{24,16},{28,20},{1,9},{5... | collective-permute-start | bytes 995336 | tf_op jit(solution)/shard_map/ppermute | solution.py:306
  326.1 20.9 %collective-permute-start.15 = (bf16[2,2,648,128]{3,2,1,0:T(8,128)(2,1)S(1)}, bf16[2,2,648,128]{3,2,1,0:T(8,128)(2,1)S(1)}, u32[]{:S(2)}, u32[]{:S(2)}) collective-permute-start(bf16[2,2,648,128]{3,2,1,0:T(8,128)(2,1)S(1)} %pad_maximum_fusion.2), channel_id=1, source_target_pairs={{0,16},{4,20},{8,24},{12,28},{16,0},{20,4},{24,8},{28,12},{1,17},{... | collective-permute-start | bytes 1990664 | tf_op jit(solution)/shard_map/ppermute | solution.py:306
Sparse Core Ops, SparseCore 0:
  25.6 44.7 all-gather.3
  72.5 20.6 all-gather.7
  95.3 30.7 all-gather.5

commit v2 on v1

v2 whole, which is shorter than its diff:
```python
import functools
import math

import jax
import jax.numpy as jnp
from jax import lax
from jax.experimental import pallas as pl
from jax.experimental.pallas import tpu as pltpu
from jax.sharding import PartitionSpec as P

H = 9
KV = 3
HD = 64
GROUPS = H // KV
KVW = KV * HD

EPS = 1e-05
THETA = 100000.0
NEGATIVE = -1e30
LANES = 128
FF_STEP = 256
VMEM_LIMIT = 60 * 1024 * 1024

BF16 = jnp.bfloat16
F32 = jnp.float32

SMEM_SPEC = pl.BlockSpec(memory_space=pltpu.SMEM)
VMEM_SPEC = pl.BlockSpec(memory_space=pltpu.VMEM)


def mm(left, right, left_dim=1, right_dim=0):
    return lax.dot_general(
        left, right, (((left_dim,), (right_dim,)), ((), ())), preferred_element_type=F32
    )


def call(kernel, outs, args, scratch=(), micros=1, smem=0):
    return pl.pallas_call(
        kernel,
        out_shape=outs,
        in_specs=[SMEM_SPEC] * smem + [VMEM_SPEC] * (len(args) - smem),
        out_specs=jax.tree.map(lambda _: VMEM_SPEC, outs),
        scratch_shapes=list(scratch),
        compiler_params=pltpu.CompilerParams(vmem_limit_bytes=VMEM_LIMIT),
        cost_estimate=pl.CostEstimate(
            flops=micros * 1_000_000_000, bytes_accessed=0, transcendentals=0
        ),
    )(*args)


def shaped(shape, dtype):
    return jax.ShapeDtypeStruct(tuple(shape), dtype)


def swap_halves(part):
    lane = lax.broadcasted_iota(jnp.int32, part.shape, 1)
    return jnp.where(
        lane % HD < HD // 2,
        pltpu.roll(part, LANES - HD // 2, axis=1),
        pltpu.roll(part, HD // 2, axis=1),
    )


def rotated(values, cosine, signed_sine, sign):
    rows, width = values.shape
    parts = []
    for start in range(0, width, LANES):
        part = values[:, start : start + LANES]
        used = part.shape[1]
        if used < LANES:
            part = jnp.concatenate([part, jnp.zeros((rows, LANES - used), F32)], -1)
        turned = part * cosine + sign * (swap_halves(part) * signed_sine)
        parts.append(turned[:, :used])
    return jnp.concatenate(parts, -1)


def stacked_heads(ref, group):
    first = group * GROUPS
    return jnp.concatenate(
        [ref[:, (first + g) * HD : (first + g + 1) * HD] for g in range(GROUPS)], 0
    )


def assembled(full, pieces, me):
    rows = pieces[0].shape[0]
    for relative, piece in enumerate(pieces):
        start = pl.multiple_of((me ^ relative) * rows, 16)
        full[pl.ds(start, rows), :] = piece[...]


def kv_kernel(
    tokens, packed, cosine, sine, normed_out, kv_out, weight_out, gains_out, owners, slice_rows
):
    step = packed.shape[0] // owners
    gains = []
    for owner in range(owners):
        start = owner * step
        weight_out[owner * slice_rows : (owner + 1) * slice_rows, :] = packed[
            start : start + slice_rows, :
        ]
        gains.append(packed[start + slice_rows : start + step, :slice_rows].astype(F32))
    gains = jnp.concatenate(gains, -1)
    gains_out[...] = gains[:8]
    values = tokens[...].astype(F32)
    scale = lax.rsqrt(jnp.mean(values * values, -1, keepdims=True) + EPS)
    normed = (values * scale * gains[0:1]).astype(BF16)
    normed_out[...] = normed
    linear = mm(normed, weight_out[...])
    kv_out[:, :KVW] = rotated(linear[:, :KVW], cosine[...], sine[...], 1.0).astype(BF16)
    kv_out[:, KVW:] = linear[:, KVW:].astype(BF16)


def query_kernel(index, normed, own, core, along, diagonal, cosine, sine, query_out, weight_out):
    assembled(weight_out, (own, core, along, diagonal), index[1])
    linear = mm(normed[...], weight_out[...])
    turned = rotated(linear, cosine[...], sine[...], 1.0) * (1.0 / math.sqrt(HD))
    query_out[...] = turned.astype(BF16)


def causal(scores, rows):
    key_pos = lax.broadcasted_iota(jnp.int32, scores.shape, 0)
    query_pos = lax.broadcasted_iota(jnp.int32, scores.shape, 1) % rows
    return jnp.where(query_pos >= key_pos, scores, NEGATIVE)


def forward_kernel(index, queries, *refs):
    pieces, (attended, lse_out, kv_all, q_scr, acc_scr, max_scr, sum_scr) = refs[:-7], refs[-7:]
    rows = queries.shape[0]
    here = index[0]
    if len(pieces) == 1:
        kv_all[...] = pieces[0][...]
    else:
        for place, piece in enumerate(pieces):
            owner = (here ^ (place % 2)) - 2 * (place // 2)

            @pl.when((owner >= 0) & (owner <= here))
            def _(owner=owner, piece=piece):
                kv_all[pl.ds(pl.multiple_of(owner * rows, rows), rows), :] = piece[...]

    for group in range(KV):
        q_scr[group] = stacked_heads(queries, group)
    acc_scr[...] = jnp.zeros_like(acc_scr)
    max_scr[...] = jnp.full_like(max_scr, NEGATIVE)
    sum_scr[...] = jnp.zeros_like(sum_scr)

    def block(j, masked):
        keys_at = pl.ds(pl.multiple_of(j * rows, rows), rows)
        for group in range(KV):
            keys = kv_all[keys_at, group * HD : (group + 1) * HD]
            values = kv_all[keys_at, KVW + group * HD : KVW + (group + 1) * HD]
            scores = mm(keys, q_scr[group], 1, 1)
            if masked:
                scores = causal(scores, rows)
            old_max = max_scr[group, 0:1, :]
            new_max = jnp.maximum(old_max, jnp.max(scores, 0, keepdims=True))
            weights = jnp.exp(scores - new_max)
            factor = jnp.exp(old_max - new_max)
            max_scr[group, 0:1, :] = new_max
            sum_scr[group, 0:1, :] = sum_scr[group, 0:1, :] * factor + jnp.sum(
                weights, 0, keepdims=True
            )
            acc_scr[group] = acc_scr[group] * factor + mm(values, weights.astype(BF16), 0, 0)

    def step(j, carry):
        block(j, False)
        return carry

    lax.fori_loop(0, here, step, 0)
    block(here, True)
    lse_out[...] = jnp.zeros_like(lse_out)
    for group in range(KV):
        total = sum_scr[group, 0:1, :]
        result = acc_scr[group] / total
        lse_out[group : group + 1, :] = max_scr[group, 0:1, :] + jnp.log(total)
        for g in range(GROUPS):
            head = group * GROUPS + g
            attended[:, head * HD : (head + 1) * HD] = result[:, g * rows : (g + 1) * rows].T


def rms_back(values, gain, grad):
    width = values.shape[-1]
    scale = lax.rsqrt(jnp.mean(values * values, -1, keepdims=True) + EPS)
    scaled = values * scale
    pulled = grad * gain
    along = jnp.sum(pulled * scaled, -1, keepdims=True) * (1.0 / width)
    return scale * (pulled - scaled * along), grad * scaled


def put_tiles(outs, me, grads, grad_lanes, first_row):
    rows = grads.shape[0] // len(outs)
    first, last = grad_lanes
    for relative, out in enumerate(outs):
        start = pl.multiple_of((me ^ relative) * rows, 16)
        for tile in range((last - first) // LANES):
            at = first + tile * LANES
            out[first_row + tile * rows : first_row + (tile + 1) * rows, :] = grads[
                pl.ds(start, rows), at : at + LANES
            ]


def ffn_kernel(
    index, tokens, attended, gains, out_grad,
    wo0, wo1, wo2, wo3, wi0, wi1, wi2, wi3, wd0, wd1, wd2, wd3,
    layer_out, middle_grad_out, attended_grad_out, mine, along, send, gain_grad,
    out_weight, in_weight, down_weight, result_scr, back_scr, tile_scr, down_scr,
):
    me = index[1]
    assembled(out_weight, (wo0, wo1, wo2, wo3), me)
    assembled(in_weight, (wi0, wi1, wi2, wi3), me)
    assembled(down_weight, (wd0, wd1, wd2, wd3), me)
    outs = (mine, send.at[0], along, send.at[1])
    gain = gains[1:2, :]
    ff = down_weight.shape[0]
    owners = len(outs)
    in_rows = in_weight.shape[0] // owners
    down_rows = ff // owners
    attended_low = attended[...].astype(BF16)
    middle = tokens[...].astype(F32) + mm(attended_low, out_weight[...])
    scale = lax.rsqrt(jnp.mean(middle * middle, -1, keepdims=True) + EPS)
    normed = (middle * scale * gain).astype(BF16)
    grad_rows = out_grad[...]
    result_scr[...] = middle
    back_scr[...] = jnp.zeros_like(back_scr)
    width = grad_rows.shape[1]

    for step in range(ff // FF_STEP):
        gate_at = slice(step * FF_STEP, (step + 1) * FF_STEP)
        up_at = slice(ff + step * FF_STEP, ff + (step + 1) * FF_STEP)
        gate = mm(normed, in_weight[:, gate_at])
        up = mm(normed, in_weight[:, up_at])
        gated = 1.0 / (1.0 + jnp.exp(-gate))
        silu = gate * gated
        hidden = (silu * up).astype(BF16)
        down = down_weight[gate_at, :]
        result_scr[...] += mm(hidden, down)
        hidden_grad = mm(grad_rows, down, 1, 1)
        gate_grad = (hidden_grad * up * (gated * (1.0 + gate * (1.0 - gated)))).astype(BF16)
        up_grad = (hidden_grad * silu).astype(BF16)
        back_scr[...] += mm(gate_grad, in_weight[:, gate_at], 1, 1) + mm(
            up_grad, in_weight[:, up_at], 1, 1
        )
        tile_scr[:, gate_at] = mm(normed, gate_grad, 0, 0).astype(BF16)
        tile_scr[:, up_at] = mm(normed, up_grad, 0, 0).astype(BF16)
        down_scr[gate_at, :width] = mm(hidden, grad_rows, 0, 0).astype(BF16)

    put_tiles(outs, me, tile_scr, (0, 2 * ff), 0)
    base = 2 * (ff // LANES) * in_rows
    whole = width // LANES * LANES
    put_tiles(outs, me, down_scr, (0, whole), base)
    base += whole // LANES * down_rows
    half = down_rows // 2
    for relative, out in enumerate(outs):
        start = pl.multiple_of((me ^ relative) * down_rows, 16)
        rest = jnp.concatenate(
            [
                down_scr[pl.ds(start, half), whole:width],
                down_scr[pl.ds(pl.multiple_of(start + half, 16), half), whole:width],
            ],
            -1,
        )
        out[base : base + half, :] = rest
    base += half

    layer_out[...] = result_scr[...].astype(BF16)
    middle_back, gain_terms = rms_back(middle, gain, back_scr[...])
    gain_grad[...] = jnp.zeros_like(gain_grad)
    gain_grad[0:1, :] = jnp.sum(gain_terms, 0, keepdims=True)
    middle_grad = middle_back + grad_rows.astype(F32)
    middle_grad_out[...] = middle_grad
    branch = middle_grad.astype(BF16)
    attended_grad_out[...] = mm(branch, out_weight[...], 1, 1).astype(BF16)
    out_weight_grad = mm(attended_low, branch, 0, 0).astype(BF16)
    wide = -(-width // LANES) * LANES
    tile_scr[:, :wide] = jnp.concatenate(
        [out_weight_grad, jnp.zeros((width, wide - width), BF16)], -1
    )
    put_tiles(outs, me, tile_scr, (0, wide), base)
    base += wide // LANES * in_rows
    for out in outs:
        out[base:, :] = jnp.zeros((out.shape[0] - base, LANES), BF16)


def backward_kernel(
    index, queries, kv_all, attended, attended_grad, lse, normed, query_weight, cosine, sine,
    kv_grads, query_weight_grad, normed_grad,
    q_scr, g_scr, delta_scr, acc_scr, query_grad_scr,
):
    rows = queries.shape[0]
    blocks = kv_all.shape[0] // rows
    here = index[0]
    for group in range(KV):
        q_scr[group] = stacked_heads(queries, group)
        grads = stacked_heads(attended_grad, group)
        g_scr[group] = grads
        terms = (grads.astype(F32) * stacked_heads(attended, group)).T
        delta_scr[group, 0:1, :] = jnp.sum(terms, 0, keepdims=True)
    acc_scr[...] = jnp.zeros_like(acc_scr)

    def block(j, masked):
        keys_at = pl.ds(pl.multiple_of(j * rows, rows), rows)
        for group in range(KV):
            key_lanes = slice(group * HD, (group + 1) * HD)
            value_lanes = slice(KVW + group * HD, KVW + (group + 1) * HD)
            keys = kv_all[keys_at, key_lanes]
            values = kv_all[keys_at, value_lanes]
            group_q = q_scr[group]
            group_g = g_scr[group]
            scores = mm(keys, group_q, 1, 1)
            if masked:
                scores = causal(scores, rows)
            prob = jnp.exp(scores - lse[group : group + 1, :])
            prob_grad = mm(values, group_g, 1, 1)
            score_grad = (prob * (prob_grad - delta_scr[group, 0:1, :])).astype(BF16)
            kv_grads[keys_at, value_lanes] = mm(prob.astype(BF16), group_g).astype(BF16)
            kv_grads[keys_at, key_lanes] = mm(score_grad, group_q).astype(BF16)
            acc_scr[group] += mm(keys, score_grad, 0, 0)

    def step(j, carry):
        block(j, False)
        return carry

    def clear(j, carry):
        keys_at = pl.ds(pl.multiple_of(j * rows, rows), rows)
        kv_grads[keys_at, :] = jnp.zeros((rows, kv_grads.shape[1]), BF16)
        return carry

    lax.fori_loop(0, here, step, 0)
    block(here, True)
    lax.fori_loop(here + 1, blocks, clear, 0)
    for group in range(KV):
        for g in range(GROUPS):
            head = group * GROUPS + g
            part = acc_scr[group, :, g * rows : (g + 1) * rows]
            query_grad_scr[:, head * HD : (head + 1) * HD] = part.T
    back = rotated(query_grad_scr[...], cosine[...], sine[...], -1.0) * (1.0 / math.sqrt(HD))
    back = back.astype(BF16)
    query_weight_grad[...] = mm(normed[...], back, 0, 0).astype(BF16)
    normed_grad[...] = mm(back, query_weight[...], 1, 1)


def tail_kernel(
    index, kv_parts, tokens, gains, normed, normed_grad, middle_grad, kv_weight, query_weight_grad,
    ffn_gain_grad, cosine, sine,
    tokens_grad, mine, along, send,
    tile_scr,
):
    me = index[1]
    rows, width = tokens.shape
    parts = kv_parts.shape[0] // rows

    def add(j, total):
        return total + kv_parts[pl.ds(pl.multiple_of(j * rows, rows), rows), :].astype(F32)

    kv_grad = lax.fori_loop(0, parts, add, jnp.zeros((rows, 2 * KVW), F32))
    key_back = rotated(kv_grad[:, :KVW], cosine[...], sine[...], -1.0)
    back = jnp.concatenate([key_back, kv_grad[:, KVW:]], -1).astype(BF16)
    wide = -(-width // LANES) * LANES
    tile_scr[:, wide : wide + 2 * KVW] = mm(normed[...], back, 0, 0).astype(BF16)
    total = normed_grad[...] + mm(back, kv_weight[...], 1, 1)
    values = tokens[...].astype(F32)
    input_grad, gain_terms = rms_back(values, gains[0:1, :], total)
    tokens_grad[...] = (middle_grad[...] + input_grad).astype(BF16)
    gain_grads = jnp.concatenate(
        [jnp.sum(gain_terms, 0, keepdims=True), ffn_gain_grad[0:1, :], jnp.zeros((6, width), F32)], 0
    )
    columns = jnp.concatenate([gain_grads.T, jnp.zeros((width, wide - width - 8), F32)], -1)
    tile_scr[:, :wide] = jnp.concatenate([query_weight_grad[...], columns.astype(BF16)], -1)
    outs = (mine, send.at[0], along, send.at[1])
    put_tiles(outs, me, tile_scr, (0, wide + 2 * KVW), 0)


def flattened(index, pieces, flat):
    if len(pieces) == 1:
        flat[...] = pieces[0][...]
        return
    here = index[0]
    count = len(pieces)
    rows = pieces[0].shape[0]
    for place, piece in enumerate(pieces):
        owner = ((here ^ (place % 2)) + (count - 2 * (place // 2))) % count
        flat[pl.ds(pl.multiple_of(owner * rows, 16), rows), :] = piece[...]


def big_out_kernel(index, *refs):
    pieces, (gate_out, up_out, down_out, out_out, flat) = refs[:-5], refs[-5:]
    flattened(index, pieces, flat)
    base = 0
    for out in (gate_out, up_out):
        rows = out.shape[0]
        for tile in range(out.shape[1] // LANES):
            out[:, tile * LANES : (tile + 1) * LANES] = flat[base : base + rows, :].astype(F32)
            base += rows
    rows, width = down_out.shape
    whole = width // LANES
    for tile in range(whole):
        down_out[:, tile * LANES : (tile + 1) * LANES] = flat[base : base + rows, :].astype(F32)
        base += rows
    half = rows // 2
    rest = flat[base : base + half, :].astype(F32)
    down_out[:half, whole * LANES :] = rest[:, : width - whole * LANES]
    down_out[half:, whole * LANES :] = rest[:, width - whole * LANES :]
    base += half
    rows = out_out.shape[0]
    for tile in range(whole):
        out_out[:, tile * LANES : (tile + 1) * LANES] = flat[base : base + rows, :].astype(F32)
        base += rows
    out_out[:, whole * LANES :] = flat[base : base + rows, : width - whole * LANES].astype(F32)


def small_out_kernel(index, *refs):
    pieces, (query_out, key_out, value_out, gain_out, flat) = refs[:-5], refs[-5:]
    flattened(index, pieces, flat)
    rows, width = query_out.shape
    whole = width // LANES
    tiles = [
        flat[tile * rows : (tile + 1) * rows, :].astype(F32) for tile in range(flat.shape[0] // rows)
    ]
    for tile in range(whole):
        query_out[:, tile * LANES : (tile + 1) * LANES] = tiles[tile]
    rest = width - whole * LANES
    query_out[:, whole * LANES :] = tiles[whole][:, :rest]
    gain_out[...] = tiles[whole][:, rest : rest + 8]
    both = jnp.concatenate(tiles[whole + 1 :], -1)
    key_out[...] = both[:, :KVW]
    value_out[...] = both[:, KVW : 2 * KVW]


def swap(value, axis, bit):
    count = lax.axis_size(axis)
    return lax.ppermute(value, axis, [(i, i ^ (1 << bit)) for i in range(count)])


def gathered_ws(value):
    along = swap(value, "ws", 1)
    return value, swap(value, "ws", 0), along, swap(along, "ws", 0)


def gathered_ctx(value, causal_only):
    count = lax.axis_size("ctx")
    if count != 8:
        return (lax.all_gather(value, "ctx", axis=0, tiled=True),)
    moved = [value]
    for by in (3, 2, 1):
        pairs = [(i, i + 2 * by) for i in range(count)]
        if causal_only:
            pairs = [(i, j) for i, j in pairs if j < count]
        moved.insert(1, lax.ppermute(value, "ctx", [(i, j % count) for i, j in pairs]))
    pieces = []
    for piece in moved:
        pieces += [piece, swap(piece, "ctx", 0)]
    return tuple(pieces)


def added(*values):
    total = values[0].astype(F32)
    for value in values[1:]:
        total = total + value.astype(F32)
    return total.astype(values[0].dtype)


def scattered_ctx(value):
    count = lax.axis_size("ctx")
    parts = lax.all_to_all(value, "ctx", split_axis=0, concat_axis=0, tiled=True)
    parts = parts.reshape(count, -1, LANES).astype(F32)
    return jnp.sum(parts, 0).astype(value.dtype)


def padded_rows(rows, count):
    return -(-rows // (16 * count)) * 16 * count


def body(
    tokens,
    attn_gain,
    query_weight,
    key_weight,
    value_weight,
    output_weight,
    ffn_gain,
    gate_weight,
    up_weight,
    down_weight,
    out_grad,
):
    seq_count, rows, width = tokens.shape
    ctx_count = lax.axis_size("ctx")
    owners = lax.axis_size("ws")
    slice_rows = query_weight.shape[0]
    ff = gate_weight.shape[1]
    wide = -(-width // LANES) * LANES
    tokens = tokens.reshape(rows, width)
    out_grad = out_grad.reshape(rows, width)
    ctx_index = lax.axis_index("ctx")
    index = jnp.stack([ctx_index, lax.axis_index("ws")]).astype(jnp.int32)

    gains = jnp.stack([attn_gain, ffn_gain])
    packed = jnp.concatenate(
        [
            jnp.concatenate([key_weight, value_weight], -1),
            jnp.pad(gains, ((0, 14), (0, 2 * KVW - slice_rows))),
        ],
        0,
    )
    packed = lax.all_gather(packed, "ws", axis=0, tiled=True)
    packed, query_weight, output_weight, in_weight, down_weight = lax.optimization_barrier(
        (
            packed,
            query_weight,
            output_weight,
            jnp.concatenate([gate_weight, up_weight], -1),
            down_weight,
        )
    )

    positions = (ctx_index * rows + jnp.arange(rows, dtype=jnp.int32)).astype(F32)
    frequency = jnp.exp(jnp.arange(HD // 2).astype(F32) * (-2.0 * math.log(THETA) / HD))
    angles = positions[:, None] * frequency[None, :]
    cosine = jnp.cos(angles)
    sine = jnp.sin(angles)
    cosine = jnp.concatenate([cosine] * 4, -1)
    sine = jnp.concatenate([-sine, sine] * 2, -1)

    normed, kv_own, full_kv, gains = call(
        functools.partial(kv_kernel, owners=owners, slice_rows=slice_rows),
        (
            shaped((rows, width), BF16),
            shaped((rows, 2 * KVW), BF16),
            shaped((width, 2 * KVW), BF16),
            shaped((8, width), F32),
        ),
        (tokens, packed, cosine, sine),
        micros=3,
    )
    query_pieces = gathered_ws(query_weight)
    kv_pieces = gathered_ctx(kv_own, True)
    out_pieces = gathered_ws(output_weight)
    in_pieces = gathered_ws(in_weight)
    down_pieces = gathered_ws(down_weight)

    queries, full_query = call(
        query_kernel,
        (shaped((rows, width), BF16), shaped((width, width), BF16)),
        (index, normed) + query_pieces + (cosine, sine),
        micros=3,
        smem=1,
    )
    attended, lse, kv_all = call(
        forward_kernel,
        (
            shaped((rows, width), F32),
            shaped((8, GROUPS * rows), F32),
            shaped((ctx_count * rows, 2 * KVW), BF16),
        ),
        (index, queries) + kv_pieces,
        scratch=(
            pltpu.VMEM((KV, GROUPS * rows, HD), BF16),
            pltpu.VMEM((KV, HD, GROUPS * rows), F32),
            pltpu.VMEM((KV, 8, GROUPS * rows), F32),
            pltpu.VMEM((KV, 8, GROUPS * rows), F32),
        ),
        micros=16,
        smem=1,
    )

    big_rows = (2 * slice_rows * ff + (ff // owners) * width + slice_rows * wide) // LANES
    big_rows = padded_rows(big_rows, ctx_count)
    layer_out, middle_grad, attended_grad, mine, along, send, ffn_gain_grad = call(
        ffn_kernel,
        (
            shaped((rows, width), BF16),
            shaped((rows, width), F32),
            shaped((rows, width), BF16),
            shaped((big_rows, LANES), BF16),
            shaped((big_rows, LANES), BF16),
            shaped((2, big_rows, LANES), BF16),
            shaped((8, width), F32),
        ),
        (index, tokens, attended, gains, out_grad) + out_pieces + in_pieces + down_pieces,
        scratch=(
            pltpu.VMEM((width, width), BF16),
            pltpu.VMEM((width, 2 * ff), BF16),
            pltpu.VMEM((ff, width), BF16),
            pltpu.VMEM((rows, width), F32),
            pltpu.VMEM((rows, width), F32),
            pltpu.VMEM((width, 2 * ff), BF16),
            pltpu.VMEM((ff, wide), BF16),
        ),
        micros=14,
        smem=1,
    )

    got = swap(send, "ws", 0)
    attended_grad, crossing = lax.optimization_barrier((attended_grad, added(along, got[1])))
    crossed = swap(crossing, "ws", 1)

    kv_grads, query_weight_grad, normed_grad = call(
        backward_kernel,
        (
            shaped((ctx_count * rows, 2 * KVW), BF16),
            shaped((width, width), BF16),
            shaped((rows, width), F32),
        ),
        (
            index, queries, kv_all, attended, attended_grad, lse, normed, full_query, cosine, sine,
        ),
        scratch=(
            pltpu.VMEM((KV, GROUPS * rows, HD), BF16),
            pltpu.VMEM((KV, GROUPS * rows, HD), BF16),
            pltpu.VMEM((KV, 8, GROUPS * rows), F32),
            pltpu.VMEM((KV, HD, GROUPS * rows), F32),
            pltpu.VMEM((rows, width), F32),
        ),
        micros=19,
        smem=1,
    )
    kv_parts = lax.all_to_all(kv_grads, "ctx", split_axis=0, concat_axis=0, tiled=True)

    big_share = scattered_ctx(added(mine, got[0], crossed))
    big_pieces = gathered_ctx(big_share, False)

    small_rows = padded_rows(slice_rows * (wide + 2 * KVW) // LANES, ctx_count)
    tokens_grad, mine, along, send = call(
        tail_kernel,
        (
            shaped((rows, width), BF16),
            shaped((small_rows, LANES), BF16),
            shaped((small_rows, LANES), BF16),
            shaped((2, small_rows, LANES), BF16),
        ),
        (
            index, kv_parts, tokens, gains, normed, normed_grad, middle_grad, full_kv,
            query_weight_grad, ffn_gain_grad, cosine, sine,
        ),
        scratch=(pltpu.VMEM((width, wide + 2 * KVW), BF16),),
        micros=4,
        smem=1,
    )
    got = swap(send, "ws", 0)
    crossed = swap(added(along, got[1]), "ws", 1)
    small_pieces = gathered_ctx(scattered_ctx(added(mine, got[0], crossed)), False)

    gate_weight_grad, up_weight_grad, down_weight_grad, output_weight_grad = call(
        big_out_kernel,
        (
            shaped(gate_weight.shape, F32),
            shaped(up_weight.shape, F32),
            shaped(down_weight.shape, F32),
            shaped(output_weight.shape, F32),
        ),
        (index,) + big_pieces,
        scratch=(pltpu.VMEM((big_rows, LANES), BF16),),
        micros=3,
        smem=1,
    )
    query_weight_grad, key_weight_grad, value_weight_grad, gain_grads = call(
        small_out_kernel,
        (
            shaped(query_weight.shape, F32),
            shaped(key_weight.shape, F32),
            shaped(value_weight.shape, F32),
            shaped((slice_rows, 8), F32),
        ),
        (index,) + small_pieces,
        scratch=(pltpu.VMEM((small_rows, LANES), BF16),),
        micros=2,
        smem=1,
    )
    return (
        layer_out.reshape(seq_count, rows, width),
        tokens_grad.reshape(seq_count, rows, width),
        gain_grads[:, 0],
        query_weight_grad,
        key_weight_grad,
        value_weight_grad,
        output_weight_grad,
        gain_grads[:, 1],
        gate_weight_grad,
        up_weight_grad,
        down_weight_grad,
    )


def solution(mesh):
    in_specs = (
        P("ws", "ctx", None),
        P("ws"),
        P("ws", None),
        P("ws", None),
        P("ws", None),
        P("ws", None),
        P("ws"),
        P("ws", None),
        P("ws", None),
        P("ws", None),
        P("ws", "ctx", None),
    )
    out_specs = (
        P("ws", "ctx", None),
        P("ws", "ctx", None),
        P("ws"),
        P("ws", None),
        P("ws", None),
        P("ws", None),
        P("ws", None),
        P("ws"),
        P("ws", None),
        P("ws", None),
        P("ws", None),
    )
    return jax.shard_map(body, mesh=mesh, in_specs=in_specs, out_specs=out_specs, check_vma=False)
```

time: 358 us -> 270 us (0.75)
  waiting for transfers between devices: 215 us -> 94.5 us
  starting transfers between devices: 27 us -> 94.3 us
  blocking collectives: 26.9 us -> 8.89 us
  between operations: 14.5 us -> 1.01 us
  Pallas kernels: 35.8 us -> 43.5 us
  local copies, waits for them, and re-layouts: 20.6 us -> 13.1 us
    ppermute x16 -> x28, waiting for transfers between devices: 110 us -> 32.9 us  [swap(): return lax.ppermute(value, axis, [(i, i ^ 1 << bit) for i in range(count)])]
    all_gather x3 -> x0, waiting for transfers between devices: 71.7 us -> none  [the longest x1 32.9 us: body(): lax.all_gather(jnp.concatenate([gate_weight, up_weight], -1), 'ws', axis=...]
    ppermute x0 -> x9, starting transfers between devices: none -> 32.6 us  [gathered_ctx(): lax.ppermute(value, 'ctx', [(i, j % count) for i, j in pairs])]
    all_to_all x0 -> x2, waiting for transfers between devices: none -> 22.9 us  [scattered_ctx(): lax.all_to_all(value, 'ctx', split_axis=0, concat_axis=0, tiled=True)]
    all_gather x3 -> x1, blocking collectives: 26.9 us -> 8.89 us  [body(): packed = lax.all_gather(packed, 'ws', axis=0, tiled=True)]
    all_to_all x1, starting transfers between devices: 16.7 us -> 32.4 us  [body(): lax.all_to_all(kv_grads, 'ctx', split_axis=0, concat_axis=0, tiled=True)]
    ppermute x16 -> x28, starting transfers between devices: 10.2 us -> 21.9 us  [swap(): return lax.ppermute(value, axis, [(i, i ^ 1 << bit) for i in range(count)])]
    pallas_call x6 -> x8, Pallas kernels: 35.8 us -> 43.5 us  [call(): pl.pallas_call(kernel, out_shape=outs, in_specs=[SMEM_SPEC] * smem + [VME...]
  transfers between devices with their start and end apart: 20 -> 40, of which waited for: 16 -> 18; matrix products, arithmetic and copies ran while one was open for 7% -> 5% of each run, Pallas kernels for 3% -> 9%
where the time goes in v2:
time: 270 us; the launch traced here: 269 us
  waiting for transfers between devices  94.5 us (35%)
  starting transfers between devices  94.3 us (35%)
  Pallas kernels  43.5 us (16%)
  other arithmetic  14.1 us (5%)
  local copies, waits for them, and re-layouts  13.1 us (5%)
  blocking collectives  8.89 us (3%)
    pallas_call x8, Pallas kernels, call(): pl.pallas_call(kernel, out_shape=outs, in_specs=[SMEM_SPEC] * smem + [VME...  43.5 us
    all_to_all x1, waiting for transfers between devices, body(): lax.all_to_all(kv_grads, 'ctx', split_axis=0, concat_axis=0, tiled=True)  33.7 us
    ppermute x28, waiting for transfers between devices, swap(): return lax.ppermute(value, axis, [(i, i ^ 1 << bit) for i in range(count)])  32.9 us
    ppermute x9, starting transfers between devices, gathered_ctx(): lax.ppermute(value, 'ctx', [(i, j % count) for i, j in pairs])  32.6 us
    all_to_all x1, starting transfers between devices, body(): lax.all_to_all(kv_grads, 'ctx', split_axis=0, concat_axis=0, tiled=True)  32.4 us
    all_to_all x2, waiting for transfers between devices, scattered_ctx(): lax.all_to_all(value, 'ctx', split_axis=0, concat_axis=0, tiled=True)  22.9 us
    ppermute x28, starting transfers between devices, swap(): return lax.ppermute(value, axis, [(i, i ^ 1 << bit) for i in range(count)])  21.9 us
    unnamed x75, local copies, waits for them, and re-layouts  9.67 us
  transfers between devices with their start and end apart: 40, of which 18 were waited for; matrix products, arithmetic and copies ran while one was open for 5% of the time, Pallas kernels for 9%

profile of v2, /device:TPU:0, one launch (start us, length us, event | category | flops | bytes accessed | tf_op | source)
XLA Modules:
  0.0 269.3 jit_solution(17075368716233629008)
XLA Ops:
  2.1 1.0 pad_maximum_fusion.3
  3.1 8.9 %all_gather.3.packed = bf16[640,384]{1,0:T(8,128)(2,1)} all-gather(bf16[160,384]{1,0:T(8,128)(2,1)S(1)} %pad_maximum_fusion.3), channel_id=1, replica_groups=mesh['ctx'=8,'ws'=4] {'ws'}, dimensions={0}, use_global_device_ids=true | all-gather | bytes 614400 | tf_op jit(solution)/shard_map/all_gather | solution.py:504
  12.0 1.2 pad_maximum_fusion.wi0
  13.2 1.2 collective-permute-start.1
  14.5 0.9 collective-permute-start.11
  15.6 1.1 collective-permute-start.14
  16.7 0.9 copy.38
  18.1 1.0 pad_maximum_fusion.1
  19.1 2.7 %shard_map.194 = (bf16[256,576]{1,0:T(8,128)(2,1)}, bf16[256,384]{1,0:T(8,128)(2,1)}, bf16[576,384]{1,0:T(8,128)(2,1)}, f32[8,576]{1,0:T(8,128)}) custom-call(bf16[256,576]{1,0:T(8,128)(2,1)} %bitcast.31, bf16[640,384]{1,0:T(8,128)(2,1)} %all_gather.3.packed, f32[256,128]{1,0:T(8,128)} %get-tuple-element.125.cosine, f32[256,128]{1,0:T(8,128)} %get-tuple-element.126.sine), custom_call_target="tpu_custom_call" | custom-call | flops 3000000000 | tf_op jit(solution)/shard_map/pallas_call | solution.py:38
  21.8 5.5 %collective-permute-start.8 = (bf16[256,384]{1,0:T(8,128)(2,1)}, bf16[256,384]{1,0:T(8,128)(2,1)S(1)}, u32[]{:S(2)}, u32[]{:S(2)}) collective-permute-start(bf16[256,384]{1,0:T(8,128)(2,1)} %get-tuple-element.53.refs_0_), channel_id=1, source_target_pairs={{0,24},{4,28},{1,25},{5,29},{2,26},{6,30},{3,27},{7,31}} | collective-permute-start | bytes 589832 | tf_op jit(solution)/shard_map/ppermute | solution.py:447
  27.3 2.0 collective-permute-start.6
  29.3 3.1 %collective-permute-start.4 = (bf16[256,384]{1,0:T(8,128)(2,1)}, bf16[256,384]{1,0:T(8,128)(2,1)}, u32[]{:S(2)}, u32[]{:S(2)}) collective-permute-start(bf16[256,384]{1,0:T(8,128)(2,1)} %get-tuple-element.53.refs_0_), channel_id=1, source_target_pairs={{0,8},{4,12},{8,16},{12,20},{16,24},{20,28},{1,9},{5,13},{9,17},{1... | collective-permute-start | bytes 589832 | tf_op jit(solution)/shard_map/ppermute | solution.py:447
  32.5 1.5 collective-permute-start.3
  35.0 2.2 collective-permute-done.6.refs_4_
  37.2 0.9 collective-permute-start.17
  38.1 0.9 copy.40
  39.6 0.9 collective-permute-done.4.refs_2_
  40.5 1.5 collective-permute-start.9
  42.5 1.5 collective-permute-start.5
  44.1 2.9 %shard_map.195 = (bf16[256,576]{1,0:T(8,128)(2,1)}, bf16[576,576]{1,0:T(8,128)(2,1)}) custom-call(s32[2]{0:T(128)} %pad_add_fusion.index, bf16[256,576]{1,0:T(8,128)(2,1)} %get-tuple-element.50.normed, bf16[144,576]{1,0:T(8,128)(2,1)} %own, bf16[144,576]{1,0:T(8,128)(2,1)} %collective-permute-done.core, bf16[144,576]{1,0:T(8,128)(2,1)} %collective-permute-done.1.along, ...), custom_call_target="tpu_custom_call" | custom-call | flops 3000000000 | tf_op jit(solution)/shard_map/pallas_call | solution.py:38
  47.0 1.6 collective-permute-done.9.refs_7_
  48.6 4.2 %collective-permute-done.7.refs_5_ = bf16[256,384]{1,0:T(8,128)(2,1)S(1)} collective-permute-done((bf16[256,384]{1,0:T(8,128)(2,1)}, bf16[256,384]{1,0:T(8,128)(2,1)S(1)}, u32[]{:S(2)}, u32[]{:S(2)}) %collective-permute-start.7) | collective-permute-done | bytes 196640 | tf_op jit(solution)/shard_map/ppermute | solution.py:430
  52.8 2.4 collective-permute-done.5.refs_3_
  56.4 4.8 %shard_map.196 = (f32[256,576]{1,0:T(8,128)}, f32[8,768]{1,0:T(8,128)}, bf16[2048,384]{1,0:T(8,128)(2,1)}) custom-call(s32[2]{0:T(128)} %pad_add_fusion.index, bf16[256,576]{1,0:T(8,128)(2,1)} %get-tuple-element.52.queries, bf16[256,384]{1,0:T(8,128)(2,1)} %get-tuple-element.53.refs_0_, bf16[256,384]{1,0:T(8,128)(2,1)} %collective-permute-done.3.refs_1_, ...), custom_call_target="tpu_custom_call" | custom-call | flops 16000000000 | tf_op jit(solution)/shard_map/pallas_call | solution.py:38
  62.2 15.2 %shard_map.197 = (bf16[256,576]{1,0:T(8,128)(2,1)}, f32[256,576]{1,0:T(8,128)}, bf16[256,576]{1,0:T(8,128)(2,1)}, bf16[6016,128]{1,0:T(8,128)(2,1)}, bf16[6016,1...) custom-call(s32[2]{0:T(128)} %pad_add_fusion.index, bf16[256,576]{1,0:T(8,128)(2,1)} %bitcast.32, ...), custom_call_target="tpu_custom_call" | custom-call | flops 14000000000 | tf_op jit(solution)/shard_map/pallas_call | solution.py:38
  77.8 5.5 %collective-permute-done.19 = bf16[2,6016,128]{2,1,0:T(8,128)(2,1)S(1)} collective-permute-done((bf16[2,6016,128]{2,1,0:T(8,128)(2,1)}, bf16[2,6016,128]{2,1,0:T(8,128)(2,1)S(1)}, u32[]{:S(2)}, u32[]{:S(2)}) %collective-permute-start.19) | collective-permute-done | bytes 3080224 | tf_op jit(solution)/shard_map/ppermute | solution.py:430
  83.3 3.0 %fusion.2 = bf16[6016,128]{1,0:T(8,128)(2,1)} fusion(bf16[6016,128]{1,0:T(8,128)(2,1)} %get-tuple-element.62, bf16[2,6016,128]{2,1,0:T(8,128)(2,1)S(1)} %collective-permute-done.19), kind=kLoop, calls=%fused_computation.4 | loop fusion | flops 3080192 | bytes 4620288 | tf_op jit(solution)/shard_map/convert_element_type | solution.py:458
  86.3 0.9 collective-permute-start.29
  87.3 7.5 %shard_map.198 = (bf16[2048,384]{1,0:T(8,128)(2,1)}, bf16[576,576]{1,0:T(8,128)(2,1)}, f32[256,576]{1,0:T(8,128)}) custom-call(s32[2]{0:T(128)} %pad_add_fusion.index, bf16[256,576]{1,0:T(8,128)(2,1)} %get-tuple-element.52.queries, bf16[2048,384]{1,0:T(8,128)(2,1)} %get-tuple-element.60.kv_all, f32[256,576]{1,0:T(8,128)} %get-tuple-element.54.attended, ...), custom_call_target="tpu_custom_call" | custom-call | flops 19000000512 | tf_op jit(solution)/shard_map/pallas_call | solution.py:38
  94.8 32.4 %all-to-all-start = ((bf16[8,256,384]{2,1,0:T(8,128)(2,1)}), bf16[8,256,384]{2,1,0:T(8,128)(2,1)}, u32[]{:S(2)}, u32[]{:S(2)}) async-start(bf16[8,256,384]{2,1,0:T(8,128)(2,1)} %bitcast.30), calls=%async_computation | async-start | bytes 3145728 | tf_op jit(solution)/shard_map/all_to_all | solution.py:616
  127.2 3.6 %fusion.1 = bf16[6016,128]{1,0:T(8,128)(2,1)} fusion(bf16[6016,128]{1,0:T(8,128)(2,1)} %collective-permute-done.29, bf16[6016,128]{1,0:T(8,128)(2,1)} %get-tuple-element.81, bf16[2,6016,128]{2,1,0:T(8,128)(2,1)S(1)} %collective-permute-done.19), kind=kLoop, calls=%fused_computation.2 | loop fusion | flops 4620288 | bytes 6160384 | tf_op jit(solution)/shard_map/convert_element_type | solution.py:458
  130.8 33.7 %all-to-all-done = bf16[8,256,384]{2,1,0:T(8,128)(2,1)} async-done(((bf16[8,256,384]{2,1,0:T(8,128)(2,1)}), bf16[8,256,384]{2,1,0:T(8,128)(2,1)}, u32[]{:S(2)}, u32[]{:S(2)}) %all-to-all-start) | async-done | bytes 1572896 | tf_op jit(solution)/shard_map/all_to_all | solution.py:616
  164.5 3.6 %all-to-all-start.2 = ((bf16[8,752,128]{2,1,0:T(8,128)(2,1)}), bf16[8,752,128]{2,1,0:T(8,128)(2,1)S(1)}, u32[]{:S(2)}, u32[]{:S(2)}) async-start(bf16[8,752,128]{2,1,0:T(8,128)(2,1)} %bitcast.13), calls=%async_computation.2 | async-start | bytes 3080192 | tf_op jit(solution)/shard_map/all_to_all | solution.py:463
  168.2 5.2 %shard_map.199 = (bf16[256,576]{1,0:T(8,128)(2,1)}, bf16[1152,128]{1,0:T(8,128)(2,1)}, bf16[1152,128]{1,0:T(8,128)(2,1)}, bf16[2,1152,128]{2,1,0:T(8,128)(2,1)}) custom-call(s32[2]{0:T(128)} %pad_add_fusion.index, bf16[2048,384]{1,0:T(8,128)(2,1)} %bitcast.7.kv_parts, bf16[256,576]{1,0:T(8,128)(2,1)} %bitcast.33, f32[8,576]{1,0:T(8,128)} %get-tuple-element.55.gains, ...), custom_call_target="tpu_custom_call" | custom-call | flops 4000000000 | tf_op jit(solution)/shard_map/pallas_call | solution.py:38
  173.3 2.2 collective-permute-done.20
  175.6 1.0 fusion.3
  176.6 1.0 collective-permute-start.21
  177.6 8.1 %collective-permute-done.21 = bf16[1152,128]{1,0:T(8,128)(2,1)S(1)} collective-permute-done((bf16[1152,128]{1,0:T(8,128)(2,1)S(1)}, bf16[1152,128]{1,0:T(8,128)(2,1)S(1)}, u32[]{:S(2)}, u32[]{:S(2)}) %collective-permute-start.21) | collective-permute-done | bytes 294944 | tf_op jit(solution)/shard_map/ppermute | solution.py:430
  185.7 1.8 fusion.5
  187.5 17.1 %all-to-all-done.2 = bf16[8,752,128]{2,1,0:T(8,128)(2,1)S(1)} async-done(((bf16[8,752,128]{2,1,0:T(8,128)(2,1)}), bf16[8,752,128]{2,1,0:T(8,128)(2,1)S(1)}, u32[]{:S(2)}, u32[]{:S(2)}) %all-to-all-start.2) | async-done | bytes 1540128 | tf_op jit(solution)/shard_map/all_to_all | solution.py:463
  204.7 3.8 %all-to-all-start.1 = ((bf16[8,144,128]{2,1,0:T(8,128)(2,1)}), bf16[8,144,128]{2,1,0:T(8,128)(2,1)S(1)}, u32[]{:S(2)}, u32[]{:S(2)}) async-start(bf16[8,144,128]{2,1,0:T(8,128)(2,1)} %bitcast.11), calls=%async_computation.1 | async-start | bytes 589824 | tf_op jit(solution)/shard_map/all_to_all | solution.py:463
  208.7 3.9 %collective-permute-start.35 = (bf16[752,128]{1,0:T(8,128)(2,1)S(1)}, bf16[752,128]{1,0:T(8,128)(2,1)S(1)}, u32[]{:S(2)}, u32[]{:S(2)}) collective-permute-start(bf16[752,128]{1,0:T(8,128)(2,1)S(1)} %reduce_sum.25.refs_0_), channel_id=1, source_target_pairs={{0,24},{4,28},{8,0},{12,4},{16,8},{20,12},{24,16},{28,20},{1,25},{... | collective-permute-start | bytes 577544 | tf_op jit(solution)/shard_map/ppermute | solution.py:447
  212.6 1.1 collective-permute-start.31
  213.7 5.7 %all-to-all-done.1 = bf16[8,144,128]{2,1,0:T(8,128)(2,1)S(1)} async-done(((bf16[8,144,128]{2,1,0:T(8,128)(2,1)}), bf16[8,144,128]{2,1,0:T(8,128)(2,1)S(1)}, u32[]{:S(2)}, u32[]{:S(2)}) %all-to-all-start.1) | async-done | bytes 294944 | tf_op jit(solution)/shard_map/all_to_all | solution.py:463
  219.5 8.7 %collective-permute-start.27 = (bf16[144,128]{1,0:T(8,128)(2,1)S(1)}, bf16[144,128]{1,0:T(8,128)(2,1)S(1)}, u32[]{:S(2)}, u32[]{:S(2)}) collective-permute-start(bf16[144,128]{1,0:T(8,128)(2,1)S(1)} %reduce_sum.24.refs_0_), channel_id=1, source_target_pairs={{0,24},{4,28},{8,0},{12,4},{16,8},{20,12},{24,16},{28,20},{1,25},{... | collective-permute-start | bytes 110600 | tf_op jit(solution)/shard_map/ppermute | solution.py:447
  228.2 1.6 collective-permute-done.27.refs_6_
  229.8 8.2 %collective-permute-start.23 = (bf16[144,128]{1,0:T(8,128)(2,1)S(1)}, bf16[144,128]{1,0:T(8,128)(2,1)S(1)}, u32[]{:S(2)}, u32[]{:S(2)}) collective-permute-start(bf16[144,128]{1,0:T(8,128)(2,1)S(1)} %reduce_sum.24.refs_0_), channel_id=1, source_target_pairs={{0,8},{4,12},{8,16},{12,20},{16,24},{20,28},{24,0},{28,4},{1,9},{5... | collective-permute-start | bytes 110600 | tf_op jit(solution)/shard_map/ppermute | solution.py:447
  238.1 1.4 collective-permute-start.22
  239.7 1.4 collective-permute-start.28
  241.1 0.9 collective-permute-done.22.refs_1_
  242.0 1.4 collective-permute-start.26
  243.8 1.3 collective-permute-start.24
  245.1 0.9 copy.44
  246.9 0.9 collective-permute-start.30
  247.8 1.1 collective-permute-start.36
  248.9 0.9 collective-permute-start.34
  249.8 1.1 collective-permute-start.32
  251.6 1.8 shard_map.200
  253.5 1.7 slice_reduce_fusion
  255.2 3.5 %collective-permute-done.36.refs_7_ = bf16[752,128]{1,0:T(8,128)(2,1)S(1)} collective-permute-done((bf16[752,128]{1,0:T(8,128)(2,1)S(1)}, bf16[752,128]{1,0:T(8,128)(2,1)S(1)}, u32[]{:S(2)}, u32[]{:S(2)}) %collective-permute-start.36) | collective-permute-done | bytes 192544 | tf_op jit(solution)/shard_map/ppermute | solution.py:430
  258.7 2.1 collective-permute-done.34.refs_5_
  260.8 2.1 collective-permute-done.32.refs_3_
  263.6 3.3 %shard_map.201 = (f32[144,1536]{1,0:T(8,128)}, f32[144,1536]{1,0:T(8,128)}, f32[384,576]{1,0:T(8,128)}, f32[144,576]{1,0:T(8,128)}) custom-call(s32[2]{0:T(128)} %pad_add_fusion.index, bf16[752,128]{1,0:T(8,128)(2,1)} %copy-done.7, bf16[752,128]{1,0:T(8,128)(2,1)} %copy-done.20, bf16[752,128]{1,0:T(8,128)(2,1)} %copy-done.19, bf16[752,128]{1,0:T(8,128)(2,1)} %copy-done.23, ...), custom_call_target="tpu_custom_call" | custom-call | flops 3000000000 | tf_op jit(solution)/shard_map/pallas_call | solution.py:38
  266.9 2.4 copy.46
  (118 shorter events, 9.8 us)
Async XLA Ops:
  0.6 13.8 %copy-start.25 = (bf16[144,576]{1,0:T(8,128)(2,1)S(1)}, bf16[144,576]{1,0:T(8,128)(2,1)}, u32[]{:S(2)}) copy-start(bf16[144,576]{1,0:T(8,128)(2,1)} %wo0) | copy-start | bytes 497668
  0.7 12.6 %copy-start.24 = (bf16[144,576]{1,0:T(8,128)(2,1)S(1)}, bf16[144,576]{1,0:T(8,128)(2,1)}, u32[]{:S(2)}) copy-start(bf16[144,576]{1,0:T(8,128)(2,1)} %own) | copy-start | bytes 497668
  0.7 16.0 %copy-start.5 = (bf16[1,256,576]{1,2,0:T(8,128)(2,1)S(1)}, bf16[1,256,576]{1,2,0:T(8,128)(2,1)}, u32[]{:S(2)}) copy-start(bf16[1,256,576]{1,2,0:T(8,128)(2,1)} %param.11) | copy-start | bytes 884740
  13.2 39.6 %copy-start = (bf16[144,3072]{1,0:T(8,128)(2,1)}, bf16[144,3072]{1,0:T(8,128)(2,1)S(1)}, u32[]{:S(2)}) copy-start(bf16[144,3072]{1,0:T(8,128)(2,1)S(1)} %pad_maximum_fusion.wi0) | copy-start | bytes 2654212
  13.2 8.6 %collective-permute-start.1 = (bf16[144,576]{1,0:T(8,128)(2,1)S(1)}, bf16[144,576]{1,0:T(8,128)(2,1)}, u32[]{:S(2)}, u32[]{:S(2)}) collective-permute-start(bf16[144,576]{1,0:T(8,128)(2,1)S(1)} %copy-done.24), channel_id=1, source_target_pairs={{0,2},{1,3},{2,0},{3,1},{4,6},{5,7},{6,4},{7,5},{8,10},{9,11},{10,... | collective-permute-start | bytes 497672 | tf_op jit(solution)/shard_map/ppermute | solution.py:430
  14.4 12.9 %collective-permute-start = (bf16[144,576]{1,0:T(8,128)(2,1)S(1)}, bf16[144,576]{1,0:T(8,128)(2,1)}, u32[]{:S(2)}, u32[]{:S(2)}) collective-permute-start(bf16[144,576]{1,0:T(8,128)(2,1)S(1)} %copy-done.24), channel_id=1, source_target_pairs={{0,1},{1,0},{2,3},{3,2},{4,5},{5,4},{6,7},{7,6},{8,9},{9,8},{10,11... | collective-permute-start | bytes 497672 | tf_op jit(solution)/shard_map/ppermute | solution.py:430
  14.5 14.8 %collective-permute-start.11 = (bf16[144,576]{1,0:T(8,128)(2,1)S(1)}, bf16[144,576]{1,0:T(8,128)(2,1)S(1)}, u32[]{:S(2)}, u32[]{:S(2)}) collective-permute-start(bf16[144,576]{1,0:T(8,128)(2,1)S(1)} %copy-done.25), channel_id=1, source_target_pairs={{0,2},{1,3},{2,0},{3,1},{4,6},{5,7},{6,4},{7,5},{8,10},{9,11},{10,... | collective-permute-start | bytes 497672 | tf_op jit(solution)/shard_map/ppermute | solution.py:430
  15.4 17.1 %collective-permute-start.10 = (bf16[144,576]{1,0:T(8,128)(2,1)S(1)}, bf16[144,576]{1,0:T(8,128)(2,1)S(1)}, u32[]{:S(2)}, u32[]{:S(2)}) collective-permute-start(bf16[144,576]{1,0:T(8,128)(2,1)S(1)} %copy-done.25), channel_id=1, source_target_pairs={{0,1},{1,0},{2,3},{3,2},{4,5},{5,4},{6,7},{7,6},{8,9},{9,8},{10,11... | collective-permute-start | bytes 497672 | tf_op jit(solution)/shard_map/ppermute | solution.py:430
  15.6 40.3 %collective-permute-start.14 = (bf16[144,3072]{1,0:T(8,128)(2,1)S(1)}, bf16[144,3072]{1,0:T(8,128)(2,1)S(1)}, u32[]{:S(2)}, u32[]{:S(2)}) collective-permute-start(bf16[144,3072]{1,0:T(8,128)(2,1)S(1)} %pad_maximum_fusion.wi0), channel_id=1, source_target_pairs={{0,2},{1,3},{2,0},{3,1},{4,6},{5,7},{6,4},{7,5},{8,10},{9,11},{10,... | collective-permute-start | bytes 2654216 | tf_op jit(solution)/shard_map/ppermute | solution.py:430
  19.1 15.6 %copy-start.2 = (bf16[384,576]{0,1:T(8,128)(2,1)S(1)}, bf16[384,576]{0,1:T(8,128)(2,1)}, u32[]{:S(2)}) copy-start(bf16[384,576]{0,1:T(8,128)(2,1)} %param.20) | copy-start | bytes 1327108
  19.1 19.0 %copy-start.6 = (bf16[1,256,576]{1,2,0:T(8,128)(2,1)S(1)}, bf16[1,256,576]{1,2,0:T(8,128)(2,1)}, u32[]{:S(2)}) copy-start(bf16[1,256,576]{1,2,0:T(8,128)(2,1)} %param.21) | copy-start | bytes 884740
  21.8 12.2 %collective-permute-start.8 = (bf16[256,384]{1,0:T(8,128)(2,1)}, bf16[256,384]{1,0:T(8,128)(2,1)S(1)}, u32[]{:S(2)}, u32[]{:S(2)}) collective-permute-start(bf16[256,384]{1,0:T(8,128)(2,1)} %get-tuple-element.53.refs_0_), channel_id=1, source_target_pairs={{0,24},{4,28},{1,25},{5,29},{2,26},{6,30},{3,27},{7,31}} | collective-permute-start | bytes 589832 | tf_op jit(solution)/shard_map/ppermute | solution.py:447
  27.3 9.9 %collective-permute-start.6 = (bf16[256,384]{1,0:T(8,128)(2,1)}, bf16[256,384]{1,0:T(8,128)(2,1)}, u32[]{:S(2)}, u32[]{:S(2)}) collective-permute-start(bf16[256,384]{1,0:T(8,128)(2,1)} %get-tuple-element.53.refs_0_), channel_id=1, source_target_pairs={{0,16},{4,20},{8,24},{12,28},{1,17},{5,21},{9,25},{13,29},{2,18},{... | collective-permute-start | bytes 589832 | tf_op jit(solution)/shard_map/ppermute | solution.py:447
  29.3 5.6 %copy-start.26 = (bf16[144,576]{1,0:T(8,128)(2,1)}, bf16[144,576]{1,0:T(8,128)(2,1)S(1)}, u32[]{:S(2)}) copy-start(bf16[144,576]{1,0:T(8,128)(2,1)S(1)} %collective-permute-done.11.wo2) | copy-start | bytes 497668
  29.3 11.2 %collective-permute-start.4 = (bf16[256,384]{1,0:T(8,128)(2,1)}, bf16[256,384]{1,0:T(8,128)(2,1)}, u32[]{:S(2)}, u32[]{:S(2)}) collective-permute-start(bf16[256,384]{1,0:T(8,128)(2,1)} %get-tuple-element.53.refs_0_), channel_id=1, source_target_pairs={{0,8},{4,12},{8,16},{12,20},{16,24},{20,28},{1,9},{5,13},{9,17},{1... | collective-permute-start | bytes 589832 | tf_op jit(solution)/shard_map/ppermute | solution.py:447
  32.5 9.6 %collective-permute-start.3 = (bf16[256,384]{1,0:T(8,128)(2,1)}, bf16[256,384]{1,0:T(8,128)(2,1)}, u32[]{:S(2)}, u32[]{:S(2)}) collective-permute-start(bf16[256,384]{1,0:T(8,128)(2,1)} %get-tuple-element.53.refs_0_), channel_id=1, source_target_pairs={{0,4},{4,0},{8,12},{12,8},{16,20},{20,16},{24,28},{28,24},{1,5},{5... | collective-permute-start | bytes 589832 | tf_op jit(solution)/shard_map/ppermute | solution.py:430
  34.7 7.9 %collective-permute-start.2 = (bf16[144,576]{1,0:T(8,128)(2,1)}, bf16[144,576]{1,0:T(8,128)(2,1)}, u32[]{:S(2)}, u32[]{:S(2)}) collective-permute-start(bf16[144,576]{1,0:T(8,128)(2,1)} %collective-permute-done.1.along), channel_id=1, source_target_pairs={{0,1},{1,0},{2,3},{3,2},{4,5},{5,4},{6,7},{7,6},{8,9},{9,8},{10,11... | collective-permute-start | bytes 497672 | tf_op jit(solution)/shard_map/ppermute | solution.py:430
  35.0 13.6 %copy-start.1 = (bf16[384,576]{1,0:T(8,128)(2,1)}, bf16[384,576]{1,0:T(8,128)(2,1)S(1)}, u32[]{:S(2)}) copy-start(bf16[384,576]{1,0:T(8,128)(2,1)S(1)} %copy.43.wd0) | copy-start | bytes 1327108
  37.2 18.7 %collective-permute-start.17 = (bf16[384,576]{1,0:T(8,128)(2,1)S(1)}, bf16[384,576]{1,0:T(8,128)(2,1)S(1)}, u32[]{:S(2)}, u32[]{:S(2)}) collective-permute-start(bf16[384,576]{1,0:T(8,128)(2,1)S(1)} %copy.43.wd0), channel_id=1, source_target_pairs={{0,2},{1,3},{2,0},{3,1},{4,6},{5,7},{6,4},{7,5},{8,10},{9,11},{10,... | collective-permute-start | bytes 1327112 | tf_op jit(solution)/shard_map/ppermute | solution.py:430
  40.5 8.0 %collective-permute-start.9 = (bf16[256,384]{1,0:T(8,128)(2,1)}, bf16[256,384]{1,0:T(8,128)(2,1)S(1)}, u32[]{:S(2)}, u32[]{:S(2)}) collective-permute-start(bf16[256,384]{1,0:T(8,128)(2,1)} %copy-done.13), channel_id=1, source_target_pairs={{0,4},{4,0},{8,12},{12,8},{16,20},{20,16},{24,28},{28,24},{1,5},{5... | collective-permute-start | bytes 589832 | tf_op jit(solution)/shard_map/ppermute | solution.py:430
  42.0 10.7 %collective-permute-start.7 = (bf16[256,384]{1,0:T(8,128)(2,1)}, bf16[256,384]{1,0:T(8,128)(2,1)S(1)}, u32[]{:S(2)}, u32[]{:S(2)}) collective-permute-start(bf16[256,384]{1,0:T(8,128)(2,1)} %collective-permute-done.6.refs_4_), channel_id=1, source_target_pairs={{0,4},{4,0},{8,12},{12,8},{16,20},{20,16},{24,28},{28,24},{1,5},{5... | collective-permute-start | bytes 589832 | tf_op jit(solution)/shard_map/ppermute | solution.py:430
  42.5 12.6 %collective-permute-start.5 = (bf16[256,384]{1,0:T(8,128)(2,1)}, bf16[256,384]{1,0:T(8,128)(2,1)S(1)}, u32[]{:S(2)}, u32[]{:S(2)}) collective-permute-start(bf16[256,384]{1,0:T(8,128)(2,1)} %collective-permute-done.4.refs_2_), channel_id=1, source_target_pairs={{0,4},{4,0},{8,12},{12,8},{16,20},{20,16},{24,28},{28,24},{1,5},{5... | collective-permute-start | bytes 589832 | tf_op jit(solution)/shard_map/ppermute | solution.py:430
  48.6 7.8 %copy-start.14 = (bf16[256,384]{1,0:T(8,128)(2,1)}, bf16[256,384]{1,0:T(8,128)(2,1)S(1)}, u32[]{:S(2)}) copy-start(bf16[256,384]{1,0:T(8,128)(2,1)S(1)} %collective-permute-done.9.refs_7_) | copy-start | bytes 589828
  48.6 12.7 %collective-permute-start.16 = (bf16[384,576]{1,0:T(8,128)(2,1)S(1)}, bf16[384,576]{1,0:T(8,128)(2,1)S(1)}, u32[]{:S(2)}, u32[]{:S(2)}) collective-permute-start(bf16[384,576]{1,0:T(8,128)(2,1)S(1)} %copy.43.wd0), channel_id=1, source_target_pairs={{0,1},{1,0},{2,3},{3,2},{4,5},{5,4},{6,7},{7,6},{8,9},{9,8},{10,11... | collective-permute-start | bytes 1327112 | tf_op jit(solution)/shard_map/ppermute | solution.py:430
  52.8 8.5 %collective-permute-start.13 = (bf16[144,3072]{1,0:T(8,128)(2,1)S(1)}, bf16[144,3072]{1,0:T(8,128)(2,1)}, u32[]{:S(2)}, u32[]{:S(2)}) collective-permute-start(bf16[144,3072]{1,0:T(8,128)(2,1)S(1)} %pad_maximum_fusion.wi0), channel_id=1, source_target_pairs={{0,1},{1,0},{2,3},{3,2},{4,5},{5,4},{6,7},{7,6},{8,9},{9,8},{10,11... | collective-permute-start | bytes 2654216 | tf_op jit(solution)/shard_map/ppermute | solution.py:430
  55.2 6.1 %collective-permute-start.12 = (bf16[144,576]{1,0:T(8,128)(2,1)}, bf16[144,576]{1,0:T(8,128)(2,1)}, u32[]{:S(2)}, u32[]{:S(2)}) collective-permute-start(bf16[144,576]{1,0:T(8,128)(2,1)} %copy-done.26), channel_id=1, source_target_pairs={{0,1},{1,0},{2,3},{3,2},{4,5},{5,4},{6,7},{7,6},{8,9},{9,8},{10,11... | collective-permute-start | bytes 497672 | tf_op jit(solution)/shard_map/ppermute | solution.py:430
  55.9 5.4 %copy-start.10 = (bf16[384,576]{1,0:T(8,128)(2,1)}, bf16[384,576]{1,0:T(8,128)(2,1)S(1)}, u32[]{:S(2)}) copy-start(bf16[384,576]{1,0:T(8,128)(2,1)S(1)} %collective-permute-done.17.wd2) | copy-start | bytes 1327108
  55.9 5.4 %collective-permute-start.18 = (bf16[384,576]{1,0:T(8,128)(2,1)S(1)}, bf16[384,576]{1,0:T(8,128)(2,1)S(1)}, u32[]{:S(2)}, u32[]{:S(2)}) collective-permute-start(bf16[384,576]{1,0:T(8,128)(2,1)S(1)} %collective-permute-done.17.wd2), channel_id=1, source_target_pairs={{0,1},{1,0},{2,3},{3,2},{4,5},{5,4},{6,7},{7,6},{8,9},{9,8},{10,11... | collective-permute-start | bytes 1327112 | tf_op jit(solution)/shard_map/ppermute | solution.py:430
  55.9 5.4 %copy-start.9 = (bf16[144,3072]{1,0:T(8,128)(2,1)}, bf16[144,3072]{1,0:T(8,128)(2,1)S(1)}, u32[]{:S(2)}) copy-start(bf16[144,3072]{1,0:T(8,128)(2,1)S(1)} %collective-permute-done.14.wi2) | copy-start | bytes 2654212
  55.9 5.4 %collective-permute-start.15 = (bf16[144,3072]{1,0:T(8,128)(2,1)S(1)}, bf16[144,3072]{1,0:T(8,128)(2,1)}, u32[]{:S(2)}, u32[]{:S(2)}) collective-permute-start(bf16[144,3072]{1,0:T(8,128)(2,1)S(1)} %collective-permute-done.14.wi2), channel_id=1, source_target_pairs={{0,1},{1,0},{2,3},{3,2},{4,5},{5,4},{6,7},{7,6},{8,9},{9,8},{10,11... | collective-permute-start | bytes 2654216 | tf_op jit(solution)/shard_map/ppermute | solution.py:430
  77.5 5.8 %collective-permute-start.19 = (bf16[2,6016,128]{2,1,0:T(8,128)(2,1)}, bf16[2,6016,128]{2,1,0:T(8,128)(2,1)S(1)}, u32[]{:S(2)}, u32[]{:S(2)}) collective-permute-start(bf16[2,6016,128]{2,1,0:T(8,128)(2,1)} %get-tuple-element.63), channel_id=1, source_target_pairs={{0,1},{1,0},{2,3},{3,2},{4,5},{5,4},{6,7},{7,6},{8,9},{9,8},{10,11... | collective-permute-start | bytes 9240584 | tf_op jit(solution)/shard_map/ppermute | solution.py:430
  86.3 40.9 %collective-permute-start.29 = (bf16[6016,128]{1,0:T(8,128)(2,1)}, bf16[6016,128]{1,0:T(8,128)(2,1)}, u32[]{:S(2)}, u32[]{:S(2)}) collective-permute-start(bf16[6016,128]{1,0:T(8,128)(2,1)} %fusion.2), channel_id=1, source_target_pairs={{0,2},{1,3},{2,0},{3,1},{4,6},{5,7},{6,4},{7,5},{8,10},{9,11},{10,... | collective-permute-start | bytes 4620296 | tf_op jit(solution)/shard_map/ppermute | solution.py:430
  94.8 69.7 %all-to-all-start = ((bf16[8,256,384]{2,1,0:T(8,128)(2,1)}), bf16[8,256,384]{2,1,0:T(8,128)(2,1)}, u32[]{:S(2)}, u32[]{:S(2)}) async-start(bf16[8,256,384]{2,1,0:T(8,128)(2,1)} %bitcast.30), calls=%async_computation | async-start | bytes 3145728 | tf_op jit(solution)/shard_map/all_to_all | solution.py:616
  164.5 40.1 %all-to-all-start.2 = ((bf16[8,752,128]{2,1,0:T(8,128)(2,1)}), bf16[8,752,128]{2,1,0:T(8,128)(2,1)S(1)}, u32[]{:S(2)}, u32[]{:S(2)}) async-start(bf16[8,752,128]{2,1,0:T(8,128)(2,1)} %bitcast.13), calls=%async_computation.2 | async-start | bytes 3080192 | tf_op jit(solution)/shard_map/all_to_all | solution.py:463
  173.3 2.2 collective-permute-start.20
  176.6 9.1 %collective-permute-start.21 = (bf16[1152,128]{1,0:T(8,128)(2,1)S(1)}, bf16[1152,128]{1,0:T(8,128)(2,1)S(1)}, u32[]{:S(2)}, u32[]{:S(2)}) collective-permute-start(bf16[1152,128]{1,0:T(8,128)(2,1)S(1)} %fusion.3), channel_id=1, source_target_pairs={{0,2},{1,3},{2,0},{3,1},{4,6},{5,7},{6,4},{7,5},{8,10},{9,11},{10,... | collective-permute-start | bytes 884744 | tf_op jit(solution)/shard_map/ppermute | solution.py:430
  187.5 57.6 %copy-start.3 = (bf16[256,576]{1,0:T(8,128)(2,1)S(1)}, bf16[256,576]{1,0:T(8,128)(2,1)}, u32[]{:S(2)}) copy-start(bf16[256,576]{1,0:T(8,128)(2,1)} %get-tuple-element.59) | copy-start | bytes 884740
  204.7 41.3 %copy-start.4 = (bf16[256,576]{1,0:T(8,128)(2,1)S(1)}, bf16[256,576]{1,0:T(8,128)(2,1)}, u32[]{:S(2)}) copy-start(bf16[256,576]{1,0:T(8,128)(2,1)} %get-tuple-element.73) | copy-start | bytes 884740
  204.7 14.8 %all-to-all-start.1 = ((bf16[8,144,128]{2,1,0:T(8,128)(2,1)}), bf16[8,144,128]{2,1,0:T(8,128)(2,1)S(1)}, u32[]{:S(2)}, u32[]{:S(2)}) async-start(bf16[8,144,128]{2,1,0:T(8,128)(2,1)} %bitcast.11), calls=%async_computation.1 | async-start | bytes 589824 | tf_op jit(solution)/shard_map/all_to_all | solution.py:463
  208.7 44.7 %copy-start.7 = (bf16[752,128]{1,0:T(8,128)(2,1)}, bf16[752,128]{1,0:T(8,128)(2,1)S(1)}, u32[]{:S(2)}) copy-start(bf16[752,128]{1,0:T(8,128)(2,1)S(1)} %reduce_sum.25.refs_0_) | copy-start | bytes 577540
  208.7 39.1 %collective-permute-start.35 = (bf16[752,128]{1,0:T(8,128)(2,1)S(1)}, bf16[752,128]{1,0:T(8,128)(2,1)S(1)}, u32[]{:S(2)}, u32[]{:S(2)}) collective-permute-start(bf16[752,128]{1,0:T(8,128)(2,1)S(1)} %reduce_sum.25.refs_0_), channel_id=1, source_target_pairs={{0,24},{4,28},{8,0},{12,4},{16,8},{20,12},{24,16},{28,20},{1,25},{... | collective-permute-start | bytes 577544 | tf_op jit(solution)/shard_map/ppermute | solution.py:447
  212.6 36.3 %collective-permute-start.33 = (bf16[752,128]{1,0:T(8,128)(2,1)S(1)}, bf16[752,128]{1,0:T(8,128)(2,1)S(1)}, u32[]{:S(2)}, u32[]{:S(2)}) collective-permute-start(bf16[752,128]{1,0:T(8,128)(2,1)S(1)} %reduce_sum.25.refs_0_), channel_id=1, source_target_pairs={{0,16},{4,20},{8,24},{12,28},{16,0},{20,4},{24,8},{28,12},{1,17},{... | collective-permute-start | bytes 577544 | tf_op jit(solution)/shard_map/ppermute | solution.py:447
  212.6 37.2 %collective-permute-start.31 = (bf16[752,128]{1,0:T(8,128)(2,1)S(1)}, bf16[752,128]{1,0:T(8,128)(2,1)S(1)}, u32[]{:S(2)}, u32[]{:S(2)}) collective-permute-start(bf16[752,128]{1,0:T(8,128)(2,1)S(1)} %reduce_sum.25.refs_0_), channel_id=1, source_target_pairs={{0,8},{4,12},{8,16},{12,20},{16,24},{20,28},{24,0},{28,4},{1,9},{5... | collective-permute-start | bytes 577544 | tf_op jit(solution)/shard_map/ppermute | solution.py:447
  219.5 31.4 %copy-start.8 = (bf16[144,128]{1,0:T(8,128)(2,1)}, bf16[144,128]{1,0:T(8,128)(2,1)S(1)}, u32[]{:S(2)}) copy-start(bf16[144,128]{1,0:T(8,128)(2,1)S(1)} %reduce_sum.24.refs_0_) | copy-start | bytes 110596
  219.5 10.3 %collective-permute-start.27 = (bf16[144,128]{1,0:T(8,128)(2,1)S(1)}, bf16[144,128]{1,0:T(8,128)(2,1)S(1)}, u32[]{:S(2)}, u32[]{:S(2)}) collective-permute-start(bf16[144,128]{1,0:T(8,128)(2,1)S(1)} %reduce_sum.24.refs_0_), channel_id=1, source_target_pairs={{0,24},{4,28},{8,0},{12,4},{16,8},{20,12},{24,16},{28,20},{1,25},{... | collective-permute-start | bytes 110600 | tf_op jit(solution)/shard_map/ppermute | solution.py:447
  228.2 9.9 %collective-permute-start.25 = (bf16[144,128]{1,0:T(8,128)(2,1)S(1)}, bf16[144,128]{1,0:T(8,128)(2,1)S(1)}, u32[]{:S(2)}, u32[]{:S(2)}) collective-permute-start(bf16[144,128]{1,0:T(8,128)(2,1)S(1)} %reduce_sum.24.refs_0_), channel_id=1, source_target_pairs={{0,16},{4,20},{8,24},{12,28},{16,0},{20,4},{24,8},{28,12},{1,17},{... | collective-permute-start | bytes 110600 | tf_op jit(solution)/shard_map/ppermute | solution.py:447
  229.8 21.1 %copy-start.28 = (bf16[144,128]{1,0:T(8,128)(2,1)}, bf16[144,128]{1,0:T(8,128)(2,1)S(1)}, u32[]{:S(2)}) copy-start(bf16[144,128]{1,0:T(8,128)(2,1)S(1)} %collective-permute-done.27.refs_6_) | copy-start | bytes 110596
  229.8 9.8 %collective-permute-start.23 = (bf16[144,128]{1,0:T(8,128)(2,1)S(1)}, bf16[144,128]{1,0:T(8,128)(2,1)S(1)}, u32[]{:S(2)}, u32[]{:S(2)}) collective-permute-start(bf16[144,128]{1,0:T(8,128)(2,1)S(1)} %reduce_sum.24.refs_0_), channel_id=1, source_target_pairs={{0,8},{4,12},{8,16},{12,20},{16,24},{20,28},{24,0},{28,4},{1,9},{5... | collective-permute-start | bytes 110600 | tf_op jit(solution)/shard_map/ppermute | solution.py:447
  238.1 12.9 %copy-start.29 = (bf16[144,128]{1,0:T(8,128)(2,1)}, bf16[144,128]{1,0:T(8,128)(2,1)S(1)}, u32[]{:S(2)}) copy-start(bf16[144,128]{1,0:T(8,128)(2,1)S(1)} %collective-permute-done.25.refs_4_) | copy-start | bytes 110596
  238.1 4.0 %collective-permute-start.22 = (bf16[144,128]{1,0:T(8,128)(2,1)S(1)}, bf16[144,128]{1,0:T(8,128)(2,1)S(1)}, u32[]{:S(2)}, u32[]{:S(2)}) collective-permute-start(bf16[144,128]{1,0:T(8,128)(2,1)S(1)} %reduce_sum.24.refs_0_), channel_id=1, source_target_pairs={{0,4},{4,0},{8,12},{12,8},{16,20},{20,16},{24,28},{28,24},{1,5},{5... | collective-permute-start | bytes 110600 | tf_op jit(solution)/shard_map/ppermute | solution.py:430
  239.7 11.3 %copy-start.30 = (bf16[144,128]{1,0:T(8,128)(2,1)}, bf16[144,128]{1,0:T(8,128)(2,1)S(1)}, u32[]{:S(2)}) copy-start(bf16[144,128]{1,0:T(8,128)(2,1)S(1)} %collective-permute-done.23.refs_2_) | copy-start | bytes 110596
  239.7 4.1 %collective-permute-start.28 = (bf16[144,128]{1,0:T(8,128)(2,1)S(1)}, bf16[144,128]{1,0:T(8,128)(2,1)S(1)}, u32[]{:S(2)}, u32[]{:S(2)}) collective-permute-start(bf16[144,128]{1,0:T(8,128)(2,1)S(1)} %collective-permute-done.27.refs_6_), channel_id=1, source_target_pairs={{0,4},{4,0},{8,12},{12,8},{16,20},{20,16},{24,28},{28,24},{1,5},{5... | collective-permute-start | bytes 110600 | tf_op jit(solution)/shard_map/ppermute | solution.py:430
  242.0 8.9 %copy-start.31 = (bf16[144,128]{1,0:T(8,128)(2,1)}, bf16[144,128]{1,0:T(8,128)(2,1)S(1)}, u32[]{:S(2)}) copy-start(bf16[144,128]{1,0:T(8,128)(2,1)S(1)} %collective-permute-done.22.refs_1_) | copy-start | bytes 110596
  242.0 4.8 %collective-permute-start.26 = (bf16[144,128]{1,0:T(8,128)(2,1)S(1)}, bf16[144,128]{1,0:T(8,128)(2,1)S(1)}, u32[]{:S(2)}, u32[]{:S(2)}) collective-permute-start(bf16[144,128]{1,0:T(8,128)(2,1)S(1)} %collective-permute-done.25.refs_4_), channel_id=1, source_target_pairs={{0,4},{4,0},{8,12},{12,8},{16,20},{20,16},{24,28},{28,24},{1,5},{5... | collective-permute-start | bytes 110600 | tf_op jit(solution)/shard_map/ppermute | solution.py:430
  243.8 7.2 %copy-start.32 = (bf16[144,128]{1,0:T(8,128)(2,1)}, bf16[144,128]{1,0:T(8,128)(2,1)S(1)}, u32[]{:S(2)}) copy-start(bf16[144,128]{1,0:T(8,128)(2,1)S(1)} %collective-permute-done.28.refs_7_) | copy-start | bytes 110596
  243.8 7.2 %collective-permute-start.24 = (bf16[144,128]{1,0:T(8,128)(2,1)S(1)}, bf16[144,128]{1,0:T(8,128)(2,1)S(1)}, u32[]{:S(2)}, u32[]{:S(2)}) collective-permute-start(bf16[144,128]{1,0:T(8,128)(2,1)S(1)} %collective-permute-done.23.refs_2_), channel_id=1, source_target_pairs={{0,4},{4,0},{8,12},{12,8},{16,20},{20,16},{24,28},{28,24},{1,5},{5... | collective-permute-start | bytes 110600 | tf_op jit(solution)/shard_map/ppermute | solution.py:430
  246.9 8.3 %collective-permute-start.30 = (bf16[752,128]{1,0:T(8,128)(2,1)S(1)}, bf16[752,128]{1,0:T(8,128)(2,1)S(1)}, u32[]{:S(2)}, u32[]{:S(2)}) collective-permute-start(bf16[752,128]{1,0:T(8,128)(2,1)S(1)} %reduce_sum.25.refs_0_), channel_id=1, source_target_pairs={{0,4},{4,0},{8,12},{12,8},{16,20},{20,16},{24,28},{28,24},{1,5},{5... | collective-permute-start | bytes 577544 | tf_op jit(solution)/shard_map/ppermute | solution.py:430
  247.8 5.6 %copy-start.17 = (bf16[752,128]{1,0:T(8,128)(2,1)}, bf16[752,128]{1,0:T(8,128)(2,1)S(1)}, u32[]{:S(2)}) copy-start(bf16[752,128]{1,0:T(8,128)(2,1)S(1)} %collective-permute-done.35.refs_6_) | copy-start | bytes 577540
  247.8 10.9 %collective-permute-start.36 = (bf16[752,128]{1,0:T(8,128)(2,1)S(1)}, bf16[752,128]{1,0:T(8,128)(2,1)S(1)}, u32[]{:S(2)}, u32[]{:S(2)}) collective-permute-start(bf16[752,128]{1,0:T(8,128)(2,1)S(1)} %collective-permute-done.35.refs_6_), channel_id=1, source_target_pairs={{0,4},{4,0},{8,12},{12,8},{16,20},{20,16},{24,28},{28,24},{1,5},{5... | collective-permute-start | bytes 577544 | tf_op jit(solution)/shard_map/ppermute | solution.py:430
  248.9 4.6 %copy-start.18 = (bf16[752,128]{1,0:T(8,128)(2,1)}, bf16[752,128]{1,0:T(8,128)(2,1)S(1)}, u32[]{:S(2)}) copy-start(bf16[752,128]{1,0:T(8,128)(2,1)S(1)} %collective-permute-done.33.refs_4_) | copy-start | bytes 577540
  248.9 11.9 %collective-permute-start.34 = (bf16[752,128]{1,0:T(8,128)(2,1)S(1)}, bf16[752,128]{1,0:T(8,128)(2,1)S(1)}, u32[]{:S(2)}, u32[]{:S(2)}) collective-permute-start(bf16[752,128]{1,0:T(8,128)(2,1)S(1)} %collective-permute-done.33.refs_4_), channel_id=1, source_target_pairs={{0,4},{4,0},{8,12},{12,8},{16,20},{20,16},{24,28},{28,24},{1,5},{5... | collective-permute-start | bytes 577544 | tf_op jit(solution)/shard_map/ppermute | solution.py:430
  249.8 13.0 %collective-permute-start.32 = (bf16[752,128]{1,0:T(8,128)(2,1)S(1)}, bf16[752,128]{1,0:T(8,128)(2,1)S(1)}, u32[]{:S(2)}, u32[]{:S(2)}) collective-permute-start(bf16[752,128]{1,0:T(8,128)(2,1)S(1)} %collective-permute-done.31.refs_2_), channel_id=1, source_target_pairs={{0,4},{4,0},{8,12},{12,8},{16,20},{20,16},{24,28},{28,24},{1,5},{5... | collective-permute-start | bytes 577544 | tf_op jit(solution)/shard_map/ppermute | solution.py:430
  255.2 7.7 %copy-start.20 = (bf16[752,128]{1,0:T(8,128)(2,1)}, bf16[752,128]{1,0:T(8,128)(2,1)S(1)}, u32[]{:S(2)}) copy-start(bf16[752,128]{1,0:T(8,128)(2,1)S(1)} %collective-permute-done.30.refs_1_) | copy-start | bytes 577540
  258.7 4.1 %copy-start.21 = (bf16[752,128]{1,0:T(8,128)(2,1)}, bf16[752,128]{1,0:T(8,128)(2,1)S(1)}, u32[]{:S(2)}) copy-start(bf16[752,128]{1,0:T(8,128)(2,1)S(1)} %collective-permute-done.36.refs_7_) | copy-start | bytes 577540
  (11 other events, 19.1 us)
